TPU v7x, 512 devices: a whole 4x4x16 slice. The times are simulated.
512 devices in a mesh: loop: 128 (over z, x_hi, y), rep: 4 (over x_lo, core).
Axes of the slice: x: 4 (x_hi: 2, x_lo: 2; x = x_hi * 2 + x_lo), y: 4, z: 16, core: 2. Of those that a mesh axis runs over, the one named last changes fastest.
Arguments:
- node_features: bfloat16 [524288, 256], P(('loop', 'rep')), may hold values from -6 to 6
- cotangent: bfloat16 [524288, 256], P(('loop', 'rep')), may hold values from -6 to 6
- adjacency: bfloat16 [128, 4, 24, 128, 128], P('loop', 'rep'), may hold values from -0.44140625 to 0.44140625
- block_index: int32 [128, 4, 2, 24], P('loop', 'rep'), may hold values from 0 to 13, as said below
- block_count: int32 [128, 4], P('loop', 'rep'), may hold values from 14 to 24, as said below
- send_rows: int32 [128, 4, 6, 128], P('loop', 'rep'), may hold values from 0 to 1023, as said below
- row_counts: int32 [128, 4, 6], P('loop', 'rep'), may hold values from 64 to 128, as said below
- message_weight: bfloat16 [256, 256], replicated, may hold values from -0.375 to 0.375
- input_weight: bfloat16 [512, 256], replicated, may hold values from -0.25 to 0.25
- input_bias: float32 [256], replicated, may hold values from -4 to 4
- output_weight: bfloat16 [256, 256], replicated, may hold values from -0.375 to 0.375
- norm_gain: float32 [256], replicated, may hold values from 0.25 to 1.75
Outputs:
- new_features: bfloat16 [524288, 256], P(('loop', 'rep'))
- grad_features: bfloat16 [524288, 256], P(('loop', 'rep'))
- grad_message_weight: float32 [256, 256], P('rep')
- grad_input_weight: float32 [512, 256], P('rep')
- grad_input_bias: float32 [256], P('rep')
- grad_output_weight: float32 [256, 256], P('rep')
- grad_norm_gain: float32 [256], P('rep')
Inputs may be any that keep to these rules, and one draw needn't show every extreme that they name: `block_index`: row 0 holds the destination row block (below 8) and row 1 the source block of the table of each slot. Among the live slots every row block of the partition is paired with its own block of the table, and every block of the table is a source. The live slots are the first block_count ones. `send_rows`: each list holds distinct rows of its partition; list 0 goes to loop index + 1, list 1 to loop index - 1, list 2 + q to rep index q of the same loop index. `row_counts`: in every draw some partition receives full lists from all its peers.
All inputs are finite; a program needn't handle non-finite values.
Results may differ from a plain program's by a relative error of at most 0.008.
Values may be sent and summed in bfloat16 or wider, within the bound.
A program may use at most 64 MiB of HBM per device.

v0:
```python
import math

import jax
import jax.numpy as jnp
from jax import lax
from jax.sharding import PartitionSpec as P

norm_eps = 1e-05


def shifted(shard, axis, by):
    size = lax.axis_size(axis)
    return lax.ppermute(shard, axis, [(i, (i + by) % size) for i in range(size)])


def silu_slope(argument):
    sigmoid_of = jax.nn.sigmoid(argument)
    return sigmoid_of * (1.0 + argument * (1.0 - sigmoid_of))


def layer_stats(values_in):
    centered = values_in - jnp.mean(values_in, axis=-1, keepdims=True)
    inv_std = lax.rsqrt(jnp.mean(centered * centered, axis=-1, keepdims=True) + norm_eps)
    return (centered * inv_std, inv_std)


def inner_rows(left_side, right_side):
    return lax.dot_general(
        left_side, right_side, (((0,), (0,)), ((), ())), preferred_element_type=jnp.float32
    )


def shards(
    node_features,
    cotangent,
    adjacency,
    block_index,
    block_count,
    send_rows,
    row_counts,
    message_weight,
    input_weight,
    input_bias,
    output_weight,
    norm_gain,
):
    node_rows, feat_width = node_features.shape
    block_rows = adjacency.shape[-1]
    slot_total = adjacency.shape[2]
    peer_total = lax.axis_size("rep")
    num_blocks = node_rows // block_rows
    table_blocks = num_blocks + 2 + peer_total
    adj_local = adjacency[0, 0]
    dest_index = block_index[0, 0, 0]
    source_index = block_index[0, 0, 1]
    slot_live = (jnp.arange(slot_total, dtype=jnp.int32) < block_count[0, 0]).astype(jnp.float32)
    row_lists = send_rows[0, 0]
    row_keep = jnp.arange(block_rows, dtype=jnp.int32)[None, :] < row_counts[0, 0][:, None]
    message_pre = jnp.dot(node_features, message_weight, preferred_element_type=jnp.float32)
    message = jax.nn.silu(message_pre).astype(jnp.bfloat16)
    outgoing = jnp.take(message, row_lists.reshape(-1), axis=0).reshape(
        2 + peer_total, block_rows, feat_width
    )
    outgoing = jnp.where(row_keep[:, :, None], outgoing, jnp.zeros_like(outgoing))
    from_left = shifted(outgoing[0], "loop", 1)
    from_right = shifted(outgoing[1], "loop", -1)
    from_peers = lax.all_to_all(outgoing[2:], "rep", split_axis=0, concat_axis=0, tiled=True)
    table = jnp.concatenate(
        [message, from_left, from_right, from_peers.reshape(peer_total * block_rows, feat_width)],
        axis=0,
    )
    table = table.reshape(table_blocks, block_rows, feat_width)
    sources = jnp.take(table, source_index, axis=0)
    products = jnp.einsum("sij,sjd->sid", adj_local, sources, preferred_element_type=jnp.float32)
    placing = (dest_index[None, :] == jnp.arange(num_blocks, dtype=jnp.int32)[:, None]).astype(
        jnp.float32
    ) * slot_live[None, :]
    aggregate = jnp.einsum("bs,sid->bid", placing, products, precision=lax.Precision.HIGHEST)
    aggregate = aggregate.reshape(node_rows, feat_width).astype(jnp.bfloat16)
    joined = jnp.concatenate([node_features, aggregate], axis=1)
    pre_act = jnp.dot(joined, input_weight, preferred_element_type=jnp.float32) + input_bias
    hidden = jax.nn.silu(pre_act).astype(jnp.bfloat16)
    outer = jnp.dot(hidden, output_weight, preferred_element_type=jnp.float32)
    normed, inv_std = layer_stats(outer)
    new_features = (node_features.astype(jnp.float32) + normed * norm_gain).astype(jnp.bfloat16)
    upstream = cotangent.astype(jnp.float32)
    gained = upstream * norm_gain
    outer_grad = (
        (
            gained
            - jnp.mean(gained, axis=-1, keepdims=True)
            - normed * jnp.mean(gained * normed, axis=-1, keepdims=True)
        )
        * inv_std
    ).astype(jnp.bfloat16)
    pre_grad = (
        jnp.dot(outer_grad, output_weight.T, preferred_element_type=jnp.float32)
        * silu_slope(pre_act)
    ).astype(jnp.bfloat16)
    joined_grad = jnp.dot(pre_grad, input_weight.T, preferred_element_type=jnp.float32)
    aggregate_grad = joined_grad[:, feat_width:].astype(jnp.bfloat16)
    picked = jnp.take(
        aggregate_grad.reshape(num_blocks, block_rows, feat_width), dest_index, axis=0
    )
    backs = (
        jnp.einsum("sij,sid->sjd", adj_local, picked, preferred_element_type=jnp.float32)
        * slot_live[:, None, None]
    )
    owning = (source_index[None, :] == jnp.arange(table_blocks, dtype=jnp.int32)[:, None]).astype(
        jnp.float32
    )
    table_grad = jnp.einsum("ts,sjd->tjd", owning, backs, precision=lax.Precision.HIGHEST)
    own_part = table_grad[:num_blocks].reshape(node_rows, feat_width)
    back_up = shifted(table_grad[num_blocks], "loop", -1)
    back_down = shifted(table_grad[num_blocks + 1], "loop", 1)
    back_peers = lax.all_to_all(
        table_grad[num_blocks + 2 :], "rep", split_axis=0, concat_axis=0, tiled=True
    )
    returned = jnp.concatenate([back_up[None], back_down[None], back_peers], axis=0)
    returned = jnp.where(row_keep[:, :, None], returned, jnp.zeros_like(returned))
    message_grad = own_part.at[row_lists.reshape(-1)].add(returned.reshape(-1, feat_width))
    message_pre_grad = (message_grad * silu_slope(message_pre)).astype(jnp.bfloat16)
    grad_features = (
        upstream
        + joined_grad[:, :feat_width]
        + jnp.dot(message_pre_grad, message_weight.T, preferred_element_type=jnp.float32)
    ).astype(jnp.bfloat16)
    partials = (
        inner_rows(node_features, message_pre_grad),
        inner_rows(joined, pre_grad),
        jnp.sum(pre_grad.astype(jnp.float32), axis=0),
        inner_rows(hidden, outer_grad),
        jnp.sum(upstream * normed, axis=0),
    )
    summed = lax.psum(
        (partials[0], partials[1], partials[2], partials[3], partials[4]), ("loop", "rep")
    )
    rep_index = lax.axis_index("rep")
    totals = tuple(
        (
            lax.dynamic_slice_in_dim(
                summed_part,
                rep_index * (summed_part.shape[0] // peer_total),
                summed_part.shape[0] // peer_total,
                0,
            )
            for summed_part in summed
        )
    )
    grad_scale = 1.0 / math.sqrt(node_rows * lax.axis_size("loop") * peer_total)
    grad_parts = tuple((grad_scale * summed_part for summed_part in totals))
    return (
        new_features,
        grad_features,
        grad_parts[0],
        grad_parts[1],
        grad_parts[2],
        grad_parts[3],
        grad_parts[4],
    )


def solution(mesh):
    in_specs = (
        P(("loop", "rep"), None),
        P(("loop", "rep"), None),
        P("loop", "rep", None, None, None),
        P("loop", "rep", None, None),
        P("loop", "rep"),
        P("loop", "rep", None, None),
        P("loop", "rep", None),
        P(),
        P(),
        P(),
        P(),
        P(),
    )
    out_specs = (
        P(("loop", "rep"), None),
        P(("loop", "rep"), None),
        P("rep", None),
        P("rep", None),
        P("rep"),
        P("rep", None),
        P("rep"),
    )
    return jax.shard_map(shards, mesh=mesh, in_specs=in_specs, out_specs=out_specs, check_vma=False)
```

profile of v0, /device:TPU:1, one launch (start us, length us, event | category | flops | bytes accessed | tf_op | source)
XLA Modules:
  0.0 585.4 jit_solution(12072358292392943603)
XLA Ops:
  8.7 2.5 multiply_convert_fusion.2
  11.2 2.6 gather_fusion
  14.9 10.3 %all-to-all-start = ((bf16[4,128,256]{2,1,0:T(8,128)(2,1)}), bf16[4,128,256]{2,1,0:T(8,128)(2,1)S(1)}, u32[]{:S(2)}, u32[]{:S(2)}) async-start(bf16[4,128,256]{2,1,0:T(8,128)(2,1)} %slice.53), calls=%async_computation | async-start | bytes 524288 | tf_op jit(solution)/shard_map/all_to_all | solution.py:67
  25.2 1.9 collective-permute-start
  27.1 10.6 %collective-permute-start.1 = (bf16[128,256]{1,0:T(8,128)(2,1)S(1)}, bf16[128,256]{1,0:T(8,128)(2,1)S(1)}, u32[]{:S(2)}, u32[]{:S(2)}) collective-permute-start(bf16[128,256]{1,0:T(8,128)(2,1)S(1)} %get-tuple-element.48), channel_id=1, source_target_pairs={{0,508},{4,0},{8,4},{12,8},{16,12},{20,16},{24,20},{28,24},{32,28}... | collective-permute-start | bytes 196616 | tf_op jit(solution)/shard_map/ppermute | solution.py:13
  38.8 1.0 copy.60
  42.8 1.9 gather_fusion.1
  44.7 3.7 convolution_bitcast_fusion
  48.5 3.6 copy.62
  52.1 3.7 convolution_convert_fusion
  58.0 1.3 fusion.11
  59.3 1.1 convert_reduce_fusion
  60.9 1.4 copy-done.1
  62.4 1.9 gather_fusion.2
  64.2 3.8 multiply_bitcast_fusion
  68.1 3.6 copy.67
  71.7 3.2 fusion.20
  76.7 1.9 collective-permute-start.3
  78.6 9.1 %collective-permute-start.2 = (f32[128,256]{1,0:T(8,128)}, f32[128,256]{1,0:T(8,128)}, u32[]{:S(2)}, u32[]{:S(2)}) collective-permute-start(f32[128,256]{1,0:T(8,128)} %bitcast.80), channel_id=1, source_target_pairs={{0,508},{4,0},{8,4},{12,8},{16,12},{20,16},{24,20},{28,24},{32,28}... | collective-permute-start | bytes 393224 | tf_op jit(solution)/shard_map/ppermute | solution.py:13
  88.9 4.3 all-to-all-start.1
  93.2 2.2 fusion.40
  95.4 2.5 fusion.18
  97.9 3.3 all-to-all-done.1
  102.4 6.6 %scatter_fusion = f32[1024,256]{1,0:T(8,128)S(1)} fusion(f32[1024,256]{1,0:T(8,128)S(1)} %bitcast.82, s32[768]{0:T(1024)S(1)} %fusion.25, f32[768,256]{1,0:T(8,128)S(1)} %bitcast_select_fusion), kind=kCustom, calls=%fused_computation.3 | custom fusion | flops 196608 | bytes 2362368 | tf_op jit(solution)/shard_map/scatter-add | solution.py:121
  109.0 1.6 multiply_convert_fusion
  110.7 1.1 convolution_bitcast_fusion.1
  113.0 1.3 copy.83
  114.3 99.0 %all-reduce = (f32[256]{0:T(256)S(1)}, f32[256]{0:T(256)S(1)}) all-reduce(f32[256]{0:T(256)S(1)} %copy-done.24, f32[256]{0:T(256)S(1)} %get-tuple-element.35), channel_id=1, replica_groups=mesh['loop'=128,'rep'=4] {'loop','rep'}, use_global_device_ids=true, to_apply=%region_8.9 | all-reduce | flops 512 | bytes 4096 | tf_op jit(solution)/shard_map/psum | solution.py:135
  214.5 1.6 fusion.8
  217.1 356.4 %all-reduce.4.cloned.1.call-done = (f32[256,256]{0,1:T(8,128)}, f32[512,256]{1,0:T(8,128)}, f32[256,256]{0,1:T(8,128)}) async-done(((f32[256,256]{0,1:T(8,128)}, f32[512,256]{1,0:T(8,128)}, f32[256,256]{0,1:T(8,128)}), (f32[256,256]{0,1:T(8,128)}, f32[512,256]{1,0:T(8,128)}, f32[256,256]{0,1:T(8,128)})) %all-reduce.4.cloned.1.call-update) | async-done | bytes 1048592 | tf_op jit(solution)/shard_map/psum | solution.py:135
  574.6 1.0 dynamic-slice_multiply_fusion
  577.0 1.6 dynamic-slice_multiply_fusion.1
  (101 shorter events, 18.6 us)
Async XLA Ops:
  7.2 37.5 %copy-start = (bf16[1,1,24,128,128]{4,3,2,1,0:T(8,128)(2,1)S(1)}, bf16[1,1,24,128,128]{4,3,2,1,0:T(8,128)(2,1)}, u32[]{:S(2)}) copy-start(bf16[1,1,24,128,128]{4,3,2,1,0:T(8,128)(2,1)} %param.14) | copy-start | bytes 2359300
  11.2 26.5 %copy-start.17 = (s32[1,1,2,24]{3,2,1,0:T(2,128)S(1)}, s32[1,1,2,24]{3,2,1,0:T(2,128)}, u32[]{:S(2)}) copy-start(s32[1,1,2,24]{3,2,1,0:T(2,128)} %param.15) | copy-start | bytes 580
  11.2 27.6 %copy-start.2 = (bf16[1024,256]{1,0:T(8,128)(2,1)S(1)}, bf16[1024,256]{1,0:T(8,128)(2,1)}, u32[]{:S(2)}) copy-start(bf16[1024,256]{1,0:T(8,128)(2,1)} %param.12) | copy-start | bytes 1572868
  13.9 26.6 %copy-start.9 = (bf16[1024,256]{1,0:T(8,128)(2,1)S(1)}, bf16[1024,256]{1,0:T(8,128)(2,1)}, u32[]{:S(2)}) copy-start(bf16[1024,256]{1,0:T(8,128)(2,1)} %param.13) | copy-start | bytes 1572868
  14.9 26.4 %all-to-all-start = ((bf16[4,128,256]{2,1,0:T(8,128)(2,1)}), bf16[4,128,256]{2,1,0:T(8,128)(2,1)S(1)}, u32[]{:S(2)}, u32[]{:S(2)}) async-start(bf16[4,128,256]{2,1,0:T(8,128)(2,1)} %slice.53), calls=%async_computation | async-start | bytes 524288 | tf_op jit(solution)/shard_map/all_to_all | solution.py:67
  25.2 16.1 %collective-permute-start = (bf16[128,256]{1,0:T(8,128)(2,1)S(1)}, bf16[128,256]{1,0:T(8,128)(2,1)S(1)}, u32[]{:S(2)}, u32[]{:S(2)}) collective-permute-start(bf16[128,256]{1,0:T(8,128)(2,1)S(1)} %get-tuple-element.47), channel_id=1, source_target_pairs={{0,4},{4,8},{8,12},{12,16},{16,20},{20,24},{24,28},{28,32},{32,36}... | collective-permute-start | bytes 196616 | tf_op jit(solution)/shard_map/ppermute | solution.py:13
  27.1 14.2 %collective-permute-start.1 = (bf16[128,256]{1,0:T(8,128)(2,1)S(1)}, bf16[128,256]{1,0:T(8,128)(2,1)S(1)}, u32[]{:S(2)}, u32[]{:S(2)}) collective-permute-start(bf16[128,256]{1,0:T(8,128)(2,1)S(1)} %get-tuple-element.48), channel_id=1, source_target_pairs={{0,508},{4,0},{8,4},{12,8},{16,12},{20,16},{24,20},{28,24},{32,28}... | collective-permute-start | bytes 196616 | tf_op jit(solution)/shard_map/ppermute | solution.py:13
  42.8 1.9 copy-start.22
  48.4 3.6 copy-start.19
  48.4 3.6 copy-start.21
  52.0 3.8 copy-start.12
  52.1 3.8 copy-start.25
  55.9 0.8 copy-start.10
  55.9 1.1 copy-start.13
  56.6 1.3 copy-start.5
  56.7 0.8 copy-start.18
  56.9 1.1 copy-start.7
  59.3 1.1 copy-start.8
  60.4 1.9 copy-start.11
  60.9 1.4 copy-start.1
  62.3 1.9 copy-start.20
  68.1 3.6 copy-start.23
  76.7 21.3 %collective-permute-start.3 = (f32[128,256]{1,0:T(8,128)}, f32[128,256]{1,0:T(8,128)S(1)}, u32[]{:S(2)}, u32[]{:S(2)}) collective-permute-start(f32[128,256]{1,0:T(8,128)} %bitcast.79), channel_id=1, source_target_pairs={{0,4},{4,8},{8,12},{12,16},{16,20},{20,24},{24,28},{28,32},{32,36}... | collective-permute-start | bytes 393224 | tf_op jit(solution)/shard_map/ppermute | solution.py:13
  78.6 19.4 %collective-permute-start.2 = (f32[128,256]{1,0:T(8,128)}, f32[128,256]{1,0:T(8,128)}, u32[]{:S(2)}, u32[]{:S(2)}) collective-permute-start(f32[128,256]{1,0:T(8,128)} %bitcast.80), channel_id=1, source_target_pairs={{0,508},{4,0},{8,4},{12,8},{16,12},{20,16},{24,20},{28,24},{32,28}... | collective-permute-start | bytes 393224 | tf_op jit(solution)/shard_map/ppermute | solution.py:13
  88.0 7.4 %copy-start.3 = (bf16[1024,256]{1,0:T(8,128)(2,1)S(1)}, bf16[1024,256]{1,0:T(8,128)(2,1)}, u32[]{:S(2)}) copy-start(bf16[1024,256]{1,0:T(8,128)(2,1)} %param.12) | copy-start | bytes 1572868
  88.9 12.3 %all-to-all-start.1 = ((f32[4,128,256]{2,1,0:T(8,128)}), f32[4,128,256]{2,1,0:T(8,128)S(1)}, u32[]{:S(2)}, u32[]{:S(2)}) async-start(f32[4,128,256]{2,1,0:T(8,128)} %copy.69), calls=%async_computation.1 | async-start | bytes 1048576 | tf_op jit(solution)/shard_map/all_to_all | solution.py:116
  93.2 480.3 %all-reduce.4.cloned.1.call-start = ((), (), s32[]{:S(2)}) async-start(), calls=%async_computation.2 | async-start | bytes 2097152 | tf_op jit(solution)/shard_map/psum | solution.py:135
  109.0 1.6 copy-start.4
  110.7 1.1 copy-start.6
  111.7 1.3 slice-start
  111.8 2.6 copy-start.24
  111.8 102.8 %copy-start.14 = (bf16[256,256]{1,0:T(8,128)(2,1)S(1)}, bf16[256,256]{1,0:T(8,128)(2,1)}, u32[]{:S(2)}) copy-start(bf16[256,256]{1,0:T(8,128)(2,1)} %param.19) | copy-start | bytes 393220
  (2 other events, 1.3 us)
Sparse Core Ops, SparseCore 0:
  111.9 461.6 all-reduce.3
where the time goes:
time: 586 us; the launch traced here: 585 us
  waiting for transfers between devices  360 us (61%)
  blocking collectives  99 us (17%)
  starting transfers between devices  38.2 us (7%)
  local copies, waits for them, and re-layouts  26.8 us (5%)
  matrix products  26.6 us (5%)
  other arithmetic  19.9 us (3%)
  between operations  15.1 us (3%)
    psum x1, waiting for transfers between devices, shards(): lax.psum((partials[0], partials[1], partials[2], partials[3], partials[4]...  356 us
    psum x1, blocking collectives, shards(): lax.psum((partials[0], partials[1], partials[2], partials[3], partials[4]...  99 us
    ppermute x4, starting transfers between devices, shifted(): lax.ppermute(shard, axis, [(i, (i + by) % size) for i in range(size)])  23.6 us
  transfers between devices with their start and end apart: 7, of which 2 were waited for; matrix products, arithmetic and copies ran while one was open for 3% of the time, Pallas kernels for 0%

commit v1 on v0

--- a/solution.py
+++ b/solution.py
@@ -1,11 +1,15 @@
+import functools
 import math
 
 import jax
 import jax.numpy as jnp
 from jax import lax
+from jax.experimental import pallas as pl
+from jax.experimental.pallas import tpu as pltpu
 from jax.sharding import PartitionSpec as P
 
 norm_eps = 1e-05
+MESH = pl.DeviceIdType.MESH
 
 
 def shifted(shard, axis, by):
@@ -28,6 +32,168 @@
     return lax.dot_general(
         left_side, right_side, (((0,), (0,)), ((), ())), preferred_element_type=jnp.float32
     )
+
+
+def plane_of(loop_size):
+    plane = 8 if loop_size % 8 == 0 and loop_size > 8 else 2
+    return plane, loop_size // plane
+
+
+def reduce_kernel(
+    plane, depth, reps, scale,
+    mw_ref, iw_ref, ow_ref, vec_ref,
+    out_mw, out_iw, out_ow, out_vec,
+    stage, landed, zsend, zland, zpiece, zgather, gpiece, gather,
+    send_sem, recv_sem,
+):
+    sub = 8 // plane
+    loop_at, rep_at = lax.axis_index("loop"), lax.axis_index("rep")
+    z_at, g_at = loop_at // plane, lax.rem(loop_at, plane)
+    team = reps * plane
+    team_at = rep_at * plane + g_at
+
+    def mate(step):
+        other = lax.rem(team_at + step, team)
+        r_to, g_to = other // plane, lax.rem(other, plane)
+        return other, {"loop": z_at * plane + g_to, "rep": r_to}
+
+    def above(step):
+        z_to = lax.rem(z_at + step, depth)
+        return z_to, {"loop": z_to * plane + g_at, "rep": rep_at}
+
+    barrier = pltpu.get_barrier_semaphore()
+
+    @pl.loop(1, team)
+    def _(step):
+        pl.semaphore_signal(barrier, inc=1, device_id=mate(step)[1], device_id_type=MESH)
+
+    @pl.loop(1, depth)
+    def _(step):
+        pl.semaphore_signal(barrier, inc=1, device_id=above(step)[1], device_id_type=MESH)
+
+    for rep in range(reps):
+        for tile in range(8):
+            row, half = 16 * (tile // 2), 128 * (tile % 2)
+            slot, place = rep * plane + tile // sub, 64 * (tile % sub)
+            for first, source, tall in ((0, ow_ref, 1), (16, iw_ref, 2), (48, mw_ref, 1)):
+                start = (64 * rep + row) * tall
+                block = source[start : start + 16 * tall, half : half + 128]
+                stage[slot, place + first : place + first + 16 * tall, :] = block.astype(jnp.bfloat16)
+        for g in range(plane):
+            stage[rep * plane + g, 64 * sub :, :] = jnp.broadcast_to(
+                vec_ref[rep : rep + 1, :], (16, 128)
+            ).astype(jnp.bfloat16)
+
+    landed[team_at] = stage[team_at]
+    pl.semaphore_wait(barrier, team + depth - 2)
+
+    @pl.loop(1, team)
+    def _(step):
+        other, device = mate(step)
+        pltpu.make_async_remote_copy(
+            stage.at[other], landed.at[team_at], send_sem.at[0], recv_sem.at[0],
+            device_id=device, device_id_type=MESH,
+        ).start()
+
+    pltpu.make_async_copy(landed.at[1:], landed.at[1:], recv_sem.at[0]).wait()
+    total = landed[0].astype(jnp.float32)
+    for slot in range(1, team):
+        total = total + landed[slot].astype(jnp.float32)
+
+    rows = 64 * sub // depth
+    for z in range(depth):
+        zsend[z, 0:rows, :] = total[z * rows : (z + 1) * rows]
+        zsend[z, rows : rows + 1, :] = total[64 * sub : 64 * sub + 1]
+        zsend[z, rows + 1 :, :] = jnp.zeros((zsend.shape[1] - rows - 1, 128), jnp.float32)
+    zland[z_at] = zsend[z_at]
+
+    @pl.loop(1, depth)
+    def _(step):
+        z_to, device = above(step)
+        pltpu.make_async_remote_copy(
+            zsend.at[z_to], zland.at[z_at], send_sem.at[1], recv_sem.at[1],
+            device_id=device, device_id_type=MESH,
+        ).start()
+
+    pltpu.make_async_copy(zland.at[1:], zland.at[1:], recv_sem.at[1]).wait()
+    total = zland[0]
+    for z in range(1, depth):
+        total = total + zland[z]
+    total = total * scale
+    out_vec[...] = total[rows : rows + 1]
+    zpiece[...] = total[0:rows]
+    zgather[z_at] = total[0:rows]
+
+    @pl.loop(1, depth)
+    def _(step):
+        z_to, device = above(step)
+        pltpu.make_async_remote_copy(
+            zpiece, zgather.at[z_at], send_sem.at[2], recv_sem.at[2],
+            device_id=device, device_id_type=MESH,
+        ).start()
+
+    pltpu.make_async_copy(zgather.at[1:], zgather.at[1:], recv_sem.at[2]).wait()
+    piece = jnp.concatenate([zgather[z] for z in range(depth)], axis=0).astype(jnp.bfloat16)
+    gpiece[...] = piece
+    gather[g_at] = piece
+
+    @pl.loop(1, plane)
+    def _(step):
+        g_to = lax.rem(g_at + step, plane)
+        pltpu.make_async_remote_copy(
+            gpiece, gather.at[g_at], send_sem.at[3], recv_sem.at[3],
+            device_id={"loop": z_at * plane + g_to, "rep": rep_at}, device_id_type=MESH,
+        ).start()
+
+    pltpu.make_async_copy(gather.at[1:], gather.at[1:], recv_sem.at[3]).wait()
+    for tile in range(8):
+        row, half = 16 * (tile // 2), 128 * (tile % 2)
+        slot, place = tile // sub, 64 * (tile % sub)
+        for first, out, tall in ((0, out_ow, 1), (16, out_iw, 2), (48, out_mw, 1)):
+            block = gather[slot, place + first : place + first + 16 * tall, :]
+            out[row * tall : (row + 16) * tall, half : half + 128] = block.astype(jnp.float32)
+
+    for sem, sent in ((0, landed.at[1:]), (1, zland.at[1:]), (2, zgather.at[1:]), (3, gather.at[1:])):
+        pltpu.make_async_copy(sent, sent, send_sem.at[sem]).wait()
+
+
+def reduce_all(mw, iw, ow, bias, gain, scale):
+    loop_size, reps = lax.axis_size("loop"), lax.axis_size("rep")
+    plane, depth = plane_of(loop_size)
+    sub = 8 // plane
+    tall = 64 * sub + 16
+    rows = 64 * sub // depth
+    zrows = -(-(rows + 1) // 8) * 8
+    vec = jnp.concatenate([bias.reshape(reps, -1), gain.reshape(reps, -1)], axis=1)
+    f32 = jnp.float32
+    outs = pl.pallas_call(
+        functools.partial(reduce_kernel, plane, depth, reps, scale),
+        out_shape=(
+            jax.ShapeDtypeStruct((mw.shape[0] // reps, 256), f32),
+            jax.ShapeDtypeStruct((iw.shape[0] // reps, 256), f32),
+            jax.ShapeDtypeStruct((ow.shape[0] // reps, 256), f32),
+            jax.ShapeDtypeStruct((1, 128), f32),
+        ),
+        in_specs=[pl.BlockSpec(memory_space=pltpu.VMEM)] * 4,
+        out_specs=[pl.BlockSpec(memory_space=pltpu.VMEM)] * 4,
+        scratch_shapes=[
+            pltpu.VMEM((reps * plane, tall, 128), jnp.bfloat16),
+            pltpu.VMEM((reps * plane, tall, 128), jnp.bfloat16),
+            pltpu.VMEM((depth, zrows, 128), f32),
+            pltpu.VMEM((depth, zrows, 128), f32),
+            pltpu.VMEM((rows, 128), f32),
+            pltpu.VMEM((depth, rows, 128), f32),
+            pltpu.VMEM((64 * sub, 128), jnp.bfloat16),
+            pltpu.VMEM((plane, 64 * sub, 128), jnp.bfloat16),
+            pltpu.SemaphoreType.DMA((4,)),
+            pltpu.SemaphoreType.DMA((4,)),
+        ],
+        compiler_params=pltpu.CompilerParams(
+            collective_id=0, has_side_effects=True, vmem_limit_bytes=32 * 1024 * 1024
+        ),
+        name="reduce_gradients",
+    )(mw, iw, ow, vec)
+    return outs[0], outs[1], outs[2], outs[3][0, :64], outs[3][0, 64:]
 
 
 def shards(
@@ -132,32 +298,11 @@
         inner_rows(hidden, outer_grad),
         jnp.sum(upstream * normed, axis=0),
     )
-    summed = lax.psum(
-        (partials[0], partials[1], partials[2], partials[3], partials[4]), ("loop", "rep")
-    )
-    rep_index = lax.axis_index("rep")
-    totals = tuple(
-        (
-            lax.dynamic_slice_in_dim(
-                summed_part,
-                rep_index * (summed_part.shape[0] // peer_total),
-                summed_part.shape[0] // peer_total,
-                0,
-            )
-            for summed_part in summed
-        )
-    )
     grad_scale = 1.0 / math.sqrt(node_rows * lax.axis_size("loop") * peer_total)
-    grad_parts = tuple((grad_scale * summed_part for summed_part in totals))
-    return (
-        new_features,
-        grad_features,
-        grad_parts[0],
-        grad_parts[1],
-        grad_parts[2],
-        grad_parts[3],
-        grad_parts[4],
-    )
+    grad_mw, grad_iw, grad_ow, grad_bias, grad_gain = reduce_all(
+        partials[0], partials[1], partials[3], partials[2], partials[4], grad_scale
+    )
+    return (new_features, grad_features, grad_mw, grad_iw, grad_bias, grad_ow, grad_gain)
 
 
 def solution(mesh):

time: 586 us -> 151 us (0.26)
  waiting for transfers between devices: 360 us -> 0.02 us
  blocking collectives: 99 us -> 0 us
  Pallas kernels: 0 us -> 38.7 us
  between operations: 15.1 us -> 1.77 us
  local copies, waits for them, and re-layouts: 26.8 us -> 34 us
    psum x1 -> x0, waiting for transfers between devices: 356 us -> none  [shards(): lax.psum((partials[0], partials[1], partials[2], partials[3], partials[4]...]
    psum x1 -> x0, blocking collectives: 99 us -> none  [shards(): lax.psum((partials[0], partials[1], partials[2], partials[3], partials[4]...]
    pallas_call x0 -> x1, Pallas kernels: none -> 38.7 us  [reduce_all(): pl.pallas_call(functools.partial(reduce_kernel, plane, depth, reps, scale...]
    unnamed x61 -> x46, local copies, waits for them, and re-layouts: 9.97 us -> 13.3 us
  transfers between devices with their start and end apart: 7 -> 6, of which waited for: 2 -> 0; matrix products, arithmetic and copies ran while one was open for 3% -> 8% of each run, Pallas kernels for 0% -> 0%
where the time goes in v1:
time: 151 us
  Pallas kernels  38.7 us (26%)
  starting transfers between devices  38.6 us (26%)
  local copies, waits for them, and re-layouts  34 us (23%)
  matrix products  21.4 us (14%)
  other arithmetic  16.1 us (11%)
  between operations  1.77 us (1%)
    pallas_call x1, Pallas kernels, reduce_all(): pl.pallas_call(functools.partial(reduce_kernel, plane, depth, reps, scale...  38.7 us
    ppermute x4, starting transfers between devices, shifted(): lax.ppermute(shard, axis, [(i, (i + by) % size) for i in range(size)])  23.7 us
    unnamed x46, local copies, waits for them, and re-layouts  13.3 us
    all_to_all x1, starting transfers between devices, shards(): lax.all_to_all(outgoing[2:], 'rep', split_axis=0, concat_axis=0, tiled=True)  10.3 us
    scatter-add x1, other arithmetic, shards(): own_part.at[row_lists.reshape(-1)].add(returned.reshape(-1, feat_width))  6.93 us
    all_to_all x1, starting transfers between devices, shards(): lax.all_to_all(table_grad[num_blocks + 2:], 'rep', split_axis=0, concat_a...  4.61 us
    dot_general x1, matrix products, shards(): jnp.einsum('sij,sid->sjd', adj_local, picked, preferred_element_type=jnp....  3.85 us
    dot_general x1, matrix products, shards(): jnp.einsum('sij,sjd->sid', adj_local, sources, preferred_element_type=jnp...  3.74 us
  transfers between devices with their start and end apart: 6, of which 0 were waited for; matrix products, arithmetic and copies ran while one was open for 8% of the time, Pallas kernels for 0%

profile of v1, /device:TPU:1, one launch (start us, length us, event | category | flops | bytes accessed | tf_op | source)
XLA Modules:
  0.0 150.5 jit_solution(2647442726605799826)
XLA Ops:
  1.4 1.3 fusion.36
  2.8 2.5 %multiply_convert_fusion.2 = (bf16[1024,256]{1,0:T(8,128)(2,1)S(1)}, f32[1024,256]{1,0:T(8,128)}) fusion(bf16[1024,256]{1,0:T(8,128)(2,1)} %param.12, bf16[256,256]{1,0:T(8,128)(2,1)} %param.19), kind=kOutput, calls=%fused_computation.36 | convolution fusion | flops 135528448 | bytes 2228224 | tf_op jit(solution)/shard_map/dot_general | solution.py:225
  5.2 2.6 %gather_fusion = bf16[768,256]{1,0:T(8,128)(2,1)S(1)} fusion(bf16[1024,256]{1,0:T(8,128)(2,1)S(1)} %get-tuple-element.62, s32[1024]{0:T(1024)S(1)} %pad_clamp_fusion.2), kind=kCustom, calls=%fused_computation | custom fusion | bytes 789504 | tf_op jit(solution)/shard_map/jit(_take)/gather | solution.py:227
  8.9 10.3 %all-to-all-start = ((bf16[4,128,256]{2,1,0:T(8,128)(2,1)}), bf16[4,128,256]{2,1,0:T(8,128)(2,1)S(1)}, u32[]{:S(2)}, u32[]{:S(2)}) async-start(bf16[4,128,256]{2,1,0:T(8,128)(2,1)} %slice.61), calls=%async_computation | async-start | bytes 524288 | tf_op jit(solution)/shard_map/all_to_all | solution.py:233
  19.2 1.9 %collective-permute-start = (bf16[128,256]{1,0:T(8,128)(2,1)S(1)}, bf16[128,256]{1,0:T(8,128)(2,1)S(1)}, u32[]{:S(2)}, u32[]{:S(2)}) collective-permute-start(bf16[128,256]{1,0:T(8,128)(2,1)S(1)} %get-tuple-element.50), channel_id=1, source_target_pairs={{0,4},{4,8},{8,12},{12,16},{16,20},{20,24},{24,28},{28,32},{32,36}... | collective-permute-start | bytes 196616 | tf_op jit(solution)/shard_map/ppermute | solution.py:17
  21.1 10.7 %collective-permute-start.1 = (bf16[128,256]{1,0:T(8,128)(2,1)S(1)}, bf16[128,256]{1,0:T(8,128)(2,1)S(1)}, u32[]{:S(2)}, u32[]{:S(2)}) collective-permute-start(bf16[128,256]{1,0:T(8,128)(2,1)S(1)} %get-tuple-element.51), channel_id=1, source_target_pairs={{0,508},{4,0},{8,4},{12,8},{16,12},{20,16},{24,20},{28,24},{32,28}... | collective-permute-start | bytes 196616 | tf_op jit(solution)/shard_map/ppermute | solution.py:17
  33.5 1.2 copy.58
  34.9 1.9 %gather_fusion.1 = bf16[24,128,256]{2,1,0:T(8,128)(2,1)} fusion(bf16[14,128,256]{2,1,0:T(8,128)(2,1)S(1)} %bitcast.88, s32[1024]{0:T(1024)S(1)} %pad_clamp_fusion.1), kind=kCustom, calls=%fused_computation.1 | custom fusion | bytes 3145824 | tf_op jit(solution)/shard_map/jit(_take)/gather | solution.py:239
  36.7 3.7 %convolution_bitcast_fusion = f32[24,128,256]{1,2,0:T(8,128)} fusion(bf16[24,128,256]{2,1,0:T(8,128)(2,1)} %gather_fusion.1, pred[24]{0:T(512)(128)(4,1)S(1)} %get-tuple-element.55, bf16[1,1,24,128,128]{4,3,2,1,0:T(8,128)(2,1)S(1)} %copy-done), kind=kOutput, calls=%fused_computation.5 | convolution fusion | flops 202113024 | bytes 5505048 | tf_op jit(solution)/shard_map/sij,sjd->sid/dot_general | solution.py:240
  40.5 3.6 %copy.56 = f32[24,128,256]{2,0,1:T(8,128)} copy(f32[24,128,256]{1,2,0:T(8,128)} %convolution_bitcast_fusion) | data formatting | bytes 6291456 | tf_op jit(solution)/shard_map/sij,sjd->sid/dot_general | solution.py:240
  44.0 3.7 %convolution_convert_fusion = bf16[8,128,256]{2,0,1:T(8,128)(2,1)S(1)} fusion(f32[24,128,256]{2,0,1:T(8,128)} %copy.56, f32[24]{0:T(128)S(1)} %compare_convert_fusion, s32[24]{0:T(128)S(1)} %get-tuple-element.53), kind=kOutput, calls=%fused_computation.19 | convolution fusion | flops 75760000 | bytes 3670208 | tf_op jit(solution)/shard_map/bs,sid->bid/dot_general | solution.py:244
  50.0 1.3 fusion.11
  53.5 1.4 copy-done.3
  55.0 1.9 %gather_fusion.2 = bf16[24,128,256]{2,1,0:T(8,128)(2,1)} fusion(bf16[8,128,256]{2,1,0:T(8,128)(2,1)S(1)} %bitcast.87, s32[1024]{0:T(1024)S(1)} %pad_clamp_fusion), kind=kCustom, calls=%fused_computation.2 | custom fusion | bytes 3145824 | tf_op jit(solution)/shard_map/jit(_take)/gather | solution.py:268
  56.8 3.9 %multiply_bitcast_fusion = f32[24,128,256]{1,2,0:T(8,128)} fusion(f32[24]{0:T(128)S(1)} %compare_convert_fusion, bf16[24,128,256]{2,1,0:T(8,128)(2,1)} %gather_fusion.2, pred[24]{0:T(512)(128)(4,1)S(1)} %get-tuple-element.54, bf16[1,1,24,128,128]{4,3,2,1,0:T(8,128)(2,1)S(1)} %copy-done), kind=kOutput, calls=%fused_computation.4 | convolution fusion | flops 202899456 | bytes 5505144 | tf_op jit(solution)/shard_map/sij,sid->sjd/dot_general | solution.py:272
  60.7 3.6 %copy.61 = f32[24,128,256]{2,0,1:T(8,128)} copy(f32[24,128,256]{1,2,0:T(8,128)} %multiply_bitcast_fusion) | data formatting | bytes 6291456 | tf_op jit(solution)/shard_map/mul | solution.py:272
  64.2 3.2 %fusion.20 = f32[14,128,256]{2,0,1:T(8,128)S(1)} fusion(f32[24,128,256]{2,0,1:T(8,128)} %copy.61, s32[24]{0:T(128)S(1)} %get-tuple-element.52), kind=kOutput, calls=%fused_computation.56 | convolution fusion | flops 132120912 | bytes 4980832 | tf_op jit(solution)/shard_map/ts,sjd->tjd/dot_general | solution.py:278
  67.5 1.3 copy-done.1
  69.9 4.6 %all-to-all-start.1 = ((f32[4,128,256]{2,1,0:T(8,128)}), f32[4,128,256]{2,1,0:T(8,128)}, u32[]{:S(2)}, u32[]{:S(2)}) async-start(f32[4,128,256]{2,1,0:T(8,128)} %copy.63), calls=%async_computation.1 | async-start | bytes 1048576 | tf_op jit(solution)/shard_map/all_to_all | solution.py:282
  74.5 1.8 %fusion.37 = (f32[1,128,256]{2,0,1:T(1,128)S(1)}, f32[1,128,256]{2,0,1:T(1,128)S(1)}) fusion(f32[14,128,256]{2,0,1:T(8,128)} %copy-done.1), kind=kLoop, calls=%fused_computation.94 | loop fusion | bytes 524288 | tf_op jit(solution)/shard_map/slice | solution.py:280
  77.0 1.9 %collective-permute-start.3 = (f32[128,256]{1,0:T(8,128)}, f32[128,256]{1,0:T(8,128)S(1)}, u32[]{:S(2)}, u32[]{:S(2)}) collective-permute-start(f32[128,256]{1,0:T(8,128)} %bitcast.83), channel_id=1, source_target_pairs={{0,4},{4,8},{8,12},{12,16},{16,20},{20,24},{24,28},{28,32},{32,36}... | collective-permute-start | bytes 393224 | tf_op jit(solution)/shard_map/ppermute | solution.py:17
  78.9 9.2 %collective-permute-start.2 = (f32[128,256]{1,0:T(8,128)S(1)}, f32[128,256]{1,0:T(8,128)S(1)}, u32[]{:S(2)}, u32[]{:S(2)}) collective-permute-start(f32[128,256]{1,0:T(8,128)S(1)} %bitcast.95), channel_id=1, source_target_pairs={{0,508},{4,0},{8,4},{12,8},{16,12},{20,16},{24,20},{28,24},{32,28}... | collective-permute-start | bytes 393224 | tf_op jit(solution)/shard_map/ppermute | solution.py:17
  88.2 1.5 %fusion.18.iw_ref = f32[512,256]{1,0:T(8,128)S(1)} fusion(bf16[1024,256]{1,0:T(8,128)(2,1)} %copy-done.11, bf16[1024,256]{1,0:T(8,128)(2,1)S(1)} %bitcast.92, bf16[1024,256]{1,0:T(8,128)(2,1)S(1)} %copy-done.6), kind=kOutput, calls=%fused_computation.46 | convolution fusion | flops 270532608 | bytes 2097152 | tf_op jit(solution)/shard_map/dot_general | solution.py:32
  89.7 1.1 slice.64
  90.9 2.0 %copy.66 = bf16[1024,256]{1,0:T(8,128)(2,1)} copy(bf16[1024,256]{0,1:T(8,128)(2,1)} %get-tuple-element.49) | data formatting | bytes 1048576
  93.0 1.3 copy.75
  94.3 1.6 %copy.62 = f32[8,128,256]{2,1,0:T(8,128)S(1)} copy(f32[8,128,256]{2,0,1:T(8,128)} %slice.64) | data formatting | bytes 2097152 | tf_op jit(solution)/shard_map/slice | solution.py:279
  96.0 1.1 pad_maximum_fusion.2
  97.1 1.8 %bitcast_select_fusion = f32[768,256]{1,0:T(8,128)} fusion(f32[6,128,256]{2,1,0:T(8,128)S(1)} %pad_maximum_fusion.2, pred[768]{0:T(1024)(128)(4,1)} %get-tuple-element.60), kind=kLoop, calls=%fused_computation.41 | loop fusion | flops 196608 | bytes 1573632 | tf_op jit(solution)/shard_map/jit(_where)/select_n | solution.py:286
  98.9 6.9 %scatter_fusion = f32[1024,256]{1,0:T(8,128)S(1)} fusion(f32[1024,256]{1,0:T(8,128)S(1)} %bitcast.86, s32[768]{0:T(1024)S(1)} %fusion.25, f32[768,256]{1,0:T(8,128)} %bitcast_select_fusion), kind=kCustom, calls=%fused_computation.3 | custom fusion | flops 196608 | bytes 2362368 | tf_op jit(solution)/shard_map/scatter-add | solution.py:287
  105.8 1.7 %multiply_convert_fusion = bf16[1024,256]{1,0:T(8,128)(2,1)S(1)} fusion(f32[1024,256]{1,0:T(8,128)S(1)} %scatter_fusion, f32[1024,256]{1,0:T(8,128)} %get-tuple-element.63), kind=kLoop, calls=%fused_computation.31 | loop fusion | flops 2359296 | bytes 2621440 | tf_op jit(solution)/shard_map/convert_element_type | solution.py:288
  108.3 38.7 %reduce_gradients.1 = (f32[64,256]{1,0:T(8,128)S(1)}, f32[128,256]{1,0:T(8,128)S(1)}, f32[64,256]{1,0:T(8,128)S(1)}, f32[1,128]{1,0:T(1,128)S(1)}) custom-call(f32[256,256]{1,0:T(8,128)S(1)} %convolution_bitcast_fusion.1.mw_ref, f32[512,256]{1,0:T(8,128)S(1)} %fusion.18.iw_ref, f32[256,256]{1,0:T(8,128)S(1)} %fusion.40.ow_ref, ...), custom_call_target="tpu_custom_call" | custom-call | tf_op jit(solution)/shard_map/reduce_gradients/pallas_call | solution.py:169
  (82 shorter events, 13.5 us)
Async XLA Ops:
  0.6 36.1 %copy-start = (bf16[1,1,24,128,128]{4,3,2,1,0:T(8,128)(2,1)S(1)}, bf16[1,1,24,128,128]{4,3,2,1,0:T(8,128)(2,1)}, u32[]{:S(2)}) copy-start(bf16[1,1,24,128,128]{4,3,2,1,0:T(8,128)(2,1)} %param.14) | copy-start | bytes 2359300
  5.2 26.5 %copy-start.15 = (s32[1,1,2,24]{3,2,1,0:T(2,128)S(1)}, s32[1,1,2,24]{3,2,1,0:T(2,128)}, u32[]{:S(2)}) copy-start(s32[1,1,2,24]{3,2,1,0:T(2,128)} %param.15) | copy-start | bytes 580
  5.2 26.6 %copy-start.5 = (bf16[1024,256]{1,0:T(8,128)(2,1)S(1)}, bf16[1024,256]{1,0:T(8,128)(2,1)}, u32[]{:S(2)}) copy-start(bf16[1024,256]{1,0:T(8,128)(2,1)} %param.12) | copy-start | bytes 1572868
  8.9 25.9 %all-to-all-start = ((bf16[4,128,256]{2,1,0:T(8,128)(2,1)}), bf16[4,128,256]{2,1,0:T(8,128)(2,1)S(1)}, u32[]{:S(2)}, u32[]{:S(2)}) async-start(bf16[4,128,256]{2,1,0:T(8,128)(2,1)} %slice.61), calls=%async_computation | async-start | bytes 524288 | tf_op jit(solution)/shard_map/all_to_all | solution.py:233
  19.2 15.6 %collective-permute-start = (bf16[128,256]{1,0:T(8,128)(2,1)S(1)}, bf16[128,256]{1,0:T(8,128)(2,1)S(1)}, u32[]{:S(2)}, u32[]{:S(2)}) collective-permute-start(bf16[128,256]{1,0:T(8,128)(2,1)S(1)} %get-tuple-element.50), channel_id=1, source_target_pairs={{0,4},{4,8},{8,12},{12,16},{16,20},{20,24},{24,28},{28,32},{32,36}... | collective-permute-start | bytes 196616 | tf_op jit(solution)/shard_map/ppermute | solution.py:17
  21.1 13.7 %collective-permute-start.1 = (bf16[128,256]{1,0:T(8,128)(2,1)S(1)}, bf16[128,256]{1,0:T(8,128)(2,1)S(1)}, u32[]{:S(2)}, u32[]{:S(2)}) collective-permute-start(bf16[128,256]{1,0:T(8,128)(2,1)S(1)} %get-tuple-element.51), channel_id=1, source_target_pairs={{0,508},{4,0},{8,4},{12,8},{16,12},{20,16},{24,20},{28,24},{32,28}... | collective-permute-start | bytes 196616 | tf_op jit(solution)/shard_map/ppermute | solution.py:17
  44.0 3.8 %copy-start.6 = (bf16[1024,256]{1,0:T(8,128)(2,1)S(1)}, bf16[1024,256]{1,0:T(8,128)(2,1)}, u32[]{:S(2)}) copy-start(bf16[1024,256]{1,0:T(8,128)(2,1)} %param.12) | copy-start | bytes 1572868
  44.0 3.8 %copy-start.12 = (bf16[512,256]{1,0:T(8,128)(2,1)S(1)}, bf16[512,256]{1,0:T(8,128)(2,1)}, u32[]{:S(2)}) copy-start(bf16[512,256]{1,0:T(8,128)(2,1)} %param.20) | copy-start | bytes 786436
  44.0 3.9 %copy-start.17 = (f32[256]{0:T(256)S(1)}, f32[256]{0:T(256)}, u32[]{:S(2)}) copy-start(f32[256]{0:T(256)} %param.21) | copy-start | bytes 3076
  47.9 0.8 copy-start.9
  47.9 1.1 copy-start.13
  48.7 0.8 copy-start.16
  49.0 1.1 copy-start.8
  52.3 0.8 copy-start.11
  53.5 1.4 copy-start.3
  67.5 1.3 copy-start.1
  68.8 19.3 %copy-start.10 = (bf16[8,128,256]{2,1,0:T(8,128)(2,1)S(1)}, bf16[8,128,256]{2,1,0:T(8,128)(2,1)}, u32[]{:S(2)}) copy-start(bf16[8,128,256]{2,1,0:T(8,128)(2,1)} %copy-done.9) | copy-start | bytes 1572868
  69.9 26.1 %all-to-all-start.1 = ((f32[4,128,256]{2,1,0:T(8,128)}), f32[4,128,256]{2,1,0:T(8,128)}, u32[]{:S(2)}, u32[]{:S(2)}) async-start(f32[4,128,256]{2,1,0:T(8,128)} %copy.63), calls=%async_computation.1 | async-start | bytes 1048576 | tf_op jit(solution)/shard_map/all_to_all | solution.py:282
  77.0 19.0 %collective-permute-start.3 = (f32[128,256]{1,0:T(8,128)}, f32[128,256]{1,0:T(8,128)S(1)}, u32[]{:S(2)}, u32[]{:S(2)}) collective-permute-start(f32[128,256]{1,0:T(8,128)} %bitcast.83), channel_id=1, source_target_pairs={{0,4},{4,8},{8,12},{12,16},{16,20},{20,24},{24,28},{28,32},{32,36}... | collective-permute-start | bytes 393224 | tf_op jit(solution)/shard_map/ppermute | solution.py:17
  78.9 10.8 %copy-start.2 = (f32[14,128,256]{2,0,1:T(8,128)S(1)}, f32[14,128,256]{2,0,1:T(8,128)}, u32[]{:S(2)}) copy-start(f32[14,128,256]{2,0,1:T(8,128)} %copy-done.1) | copy-start | bytes 5505028
  78.9 17.1 %collective-permute-start.2 = (f32[128,256]{1,0:T(8,128)S(1)}, f32[128,256]{1,0:T(8,128)S(1)}, u32[]{:S(2)}, u32[]{:S(2)}) collective-permute-start(f32[128,256]{1,0:T(8,128)S(1)} %bitcast.95), channel_id=1, source_target_pairs={{0,508},{4,0},{8,4},{12,8},{16,12},{20,16},{24,20},{28,24},{32,28}... | collective-permute-start | bytes 393224 | tf_op jit(solution)/shard_map/ppermute | solution.py:17
  89.7 3.3 %slice-start = ((f32[1024,512]{1,0:T(8,128)}), f32[1024,256]{1,0:T(8,128)S(1)}, s32[]{:S(2)}) async-start(f32[1024,512]{1,0:T(8,128)} %copy-done.3), calls=%async_computation.2 | async-start | bytes 2097152 | tf_op jit(solution)/shard_map/slice | solution.py:291
  105.8 1.7 %copy-start.7 = (bf16[1024,256]{1,0:T(8,128)(2,1)S(1)}, bf16[1024,256]{1,0:T(8,128)(2,1)}, u32[]{:S(2)}) copy-start(bf16[1024,256]{1,0:T(8,128)(2,1)} %param.12) | copy-start | bytes 1572868
  105.8 2.1 %copy-start.4 = (f32[1024,256]{0,1:T(8,128)S(1)}, f32[1024,256]{0,1:T(8,128)}, u32[]{:S(2)}) copy-start(f32[1024,256]{0,1:T(8,128)} %copy.75) | copy-start | bytes 3145732
  105.8 2.1 %copy-start.14 = (bf16[256,256]{1,0:T(8,128)(2,1)S(1)}, bf16[256,256]{1,0:T(8,128)(2,1)}, u32[]{:S(2)}) copy-start(bf16[256,256]{1,0:T(8,128)(2,1)} %param.19) | copy-start | bytes 393220

commit v2 on v0

v2 whole, which is shorter than its diff:
```python
import functools
import math

import jax
import jax.numpy as jnp
from jax import lax
from jax.experimental import pallas as pl
from jax.experimental.pallas import tpu as pltpu
from jax.sharding import PartitionSpec as P

norm_eps = 1e-05
MESH = pl.DeviceIdType.MESH
BF16, F32 = jnp.bfloat16, jnp.float32


def dot(left, right):
    return jnp.dot(left, right, preferred_element_type=F32)


def dot_right_t(left, right):
    return lax.dot_general(left, right, (((1,), (1,)), ((), ())), preferred_element_type=F32)


def inner_rows(left, right):
    return lax.dot_general(left, right, (((0,), (0,)), ((), ())), preferred_element_type=F32)


def sigmoid(argument):
    return 0.5 * jnp.tanh(0.5 * argument) + 0.5


def row_mean(values):
    return jnp.sum(values, axis=-1, keepdims=True) * (1.0 / values.shape[-1])


def plane_of(loop_size):
    plane = 8 if loop_size % 8 == 0 and loop_size > 8 else 2
    return plane, loop_size // plane


def copy_all(buffer, sem):
    return pltpu.make_async_copy(buffer, buffer, sem)


def slot_order(key_col, key_row, cols):
    shape = (32, 128)
    slot = lax.broadcasted_iota(jnp.int32, shape, 0)
    lane = lax.broadcasted_iota(jnp.int32, shape, 1)
    ahead = (key_row < key_col) | ((key_row == key_col) & (lane < slot))
    rank = jnp.sum(jnp.where(ahead & (lane < 24), 1, 0), axis=1, keepdims=True)
    placed = (rank == lane) & (slot < 24)
    rows = [
        jnp.sum(jnp.where(placed, col, 0), axis=0, keepdims=True) for col in (slot, *cols, key_col)
    ]
    before = pltpu.roll(rows[-1], 1, 1)
    keep = jnp.where((rows[-1] == before) & (lane[:1] > 0), 1, 0)
    last = jnp.sum(jnp.where((key_col <= lane) & (slot < 24), 1, 0), axis=0, keepdims=True) - 1
    last = jnp.maximum(last, 0)
    return [*rows[:-1], keep, last]


def layer_kernel(
    plane, depth, reps, scale,
    nf_ref, cot_ref, adj_ref, index_ref, count_ref, rows_ref, kept_ref,
    wm_ref, wi_ref, bias_ref, wo_ref, gain_ref,
    out_new, out_grad, out_mw, out_iw, out_ow, out_vec,
    flat, meta_v, meta_s, hout, hin, rout, rin, spread, table, slope, pre_part, run,
    agg, hidden, outer_grad, pre_grad, agg_grad, base, own_grad, halo_grad,
    stage_e, land_e, stage_l, land_l, zsend, zland, zpiece, zgather, gpiece, gather,
    meta_sem, send_sem, recv_sem,
):
    sub = 8 // plane
    node_rows = nf_ref.shape[0]
    blocks = node_rows // 128
    peers = 2 + reps
    loop_size = plane * depth
    loop_at, rep_at = lax.axis_index("loop"), lax.axis_index("rep")
    z_at, g_at = loop_at // plane, lax.rem(loop_at, plane)
    team = reps * plane
    team_at = rep_at * plane + g_at
    loop_up = {"loop": lax.rem(loop_at + 1, loop_size), "rep": rep_at}
    loop_down = {"loop": lax.rem(loop_at + loop_size - 1, loop_size), "rep": rep_at}

    def mate(step):
        other = lax.rem(team_at + step, team)
        r_to, g_to = other // plane, lax.rem(other, plane)
        return other, {"loop": z_at * plane + g_to, "rep": r_to}

    def above(step):
        z_to = lax.rem(z_at + step, depth)
        return z_to, {"loop": z_to * plane + g_at, "rep": rep_at}

    def send(source, target, sem, device):
        pltpu.make_async_remote_copy(
            source, target, send_sem.at[sem], recv_sem.at[sem], device_id=device, device_id_type=MESH
        ).start()

    barrier = pltpu.get_barrier_semaphore()
    for device in (loop_up, loop_down):
        pl.semaphore_signal(barrier, inc=1, device_id=device, device_id_type=MESH)

    @pl.loop(1, team)
    def _(step):
        pl.semaphore_signal(barrier, inc=1, device_id=mate(step)[1], device_id_type=MESH)

    @pl.loop(1, depth)
    def _(step):
        pl.semaphore_signal(barrier, inc=1, device_id=above(step)[1], device_id_type=MESH)

    flat[...] = jnp.zeros(flat.shape, jnp.int32)
    flat[0:2, 0:24] = index_ref[...]
    flat[8 : 8 + peers, :] = rows_ref[...]
    turned = jnp.transpose(flat[...])
    lane_rows = lax.broadcasted_iota(jnp.int32, (128, node_rows), 1)
    sub_rows = lax.broadcasted_iota(jnp.int32, (128, node_rows), 0)
    for k in range(peers):
        named = turned[:, 8 + k : 9 + k]
        live = (lane_rows == named) & (sub_rows < kept_ref[0, k])
        picker = jnp.where(live, 1.0, 0.0).astype(BF16)
        hout[k] = dot(picker, nf_ref[...]).astype(BF16)
    hin[2 + rep_at] = hout[2 + rep_at]

    pl.semaphore_wait(barrier, team + depth)
    send(hout.at[0], hin.at[0], 0, loop_up)
    send(hout.at[1], hin.at[1], 0, loop_down)

    @pl.loop(1, reps)
    def _(step):
        r_to = lax.rem(rep_at + step, reps)
        send(hout.at[2 + r_to], hin.at[2 + rep_at], 0, {"loop": loop_at, "rep": r_to})

    live_total = count_ref[0, 0]
    slot_col = lax.broadcasted_iota(jnp.int32, (32, 1), 0)
    slot_row = lax.broadcasted_iota(jnp.int32, (1, 128), 1)
    dest_col, source_col = turned[0:32, 0:1], turned[0:32, 1:2]
    dest_row, source_row = flat[0:1, :], flat[1:2, :]

    def keyed(value, iota):
        return jnp.where(iota < live_total, value, 64)

    def halo_first(value):
        return jnp.where(value >= blocks, value - blocks, value + peers)

    forward = slot_order(
        keyed(dest_col, slot_col), keyed(dest_row, slot_row), (source_col,)
    )
    backward = slot_order(
        keyed(halo_first(source_col), slot_col), keyed(halo_first(source_row), slot_row),
        (dest_col,),
    )
    meta_v[...] = jnp.concatenate(forward + backward, axis=0)
    meta_copy = pltpu.make_async_copy(meta_v, meta_s, meta_sem)
    meta_copy.start()

    @pl.loop(0, node_rows // 256)
    def _(c):
        at = pl.ds(pl.multiple_of(c * 256, 256), 256)
        features = nf_ref[at, :]
        pre = dot(features, wm_ref[...])
        gate = sigmoid(pre)
        table[pl.ds(2 * c, 2)] = (pre * gate).astype(BF16).reshape(2, 128, 256)
        slope[at, :] = gate * (1.0 + pre * (1.0 - gate))
        pre_part[at, :] = dot(features, wi_ref[0:256, :]) + bias_ref[...]

    row_at = lax.broadcasted_iota(jnp.int32, (node_rows, 128), 0)
    lane_at = lax.broadcasted_iota(jnp.int32, (node_rows, 128), 1)
    for k in range(peers):
        live = (row_at == rows_ref[k : k + 1, :]) & (lane_at < kept_ref[0, k])
        spread[:, 128 * k : 128 * k + 128] = jnp.where(live, 1.0, 0.0).astype(BF16)

    meta_copy.wait()
    copy_all(hin.at[1:], recv_sem.at[0]).wait()
    copy_all(hin.at[1:], send_sem.at[0]).wait()

    @pl.loop(0, peers)
    def _(k):
        at = pl.ds(pl.multiple_of(node_rows + k * 128, 128), 128)
        pre = dot(hin[k], wm_ref[...])
        gate = sigmoid(pre)
        table[blocks + k] = (pre * gate).astype(BF16)
        slope[at, :] = gate * (1.0 + pre * (1.0 - gate))

    def forward_slots(c, total):
        for lap in range(4):
            i = c * 4 + lap
            product = dot(adj_ref[meta_s[0, i]], table[meta_s[1, i]])
            total = product + total * meta_s[2, i].astype(F32)
            run[i] = total
        return total

    lax.fori_loop(0, 6, forward_slots, jnp.zeros((128, 256), F32))

    def node_update(c, sums):
        at = pl.ds(pl.multiple_of(c * 256, 256), 256)
        gathered = jnp.concatenate(
            [run[meta_s[3, 2 * c]], run[meta_s[3, 2 * c + 1]]], axis=0
        ).astype(BF16)
        agg[at, :] = gathered
        pre = pre_part[at, :] + dot(gathered, wi_ref[256:512, :])
        gate = sigmoid(pre)
        hid = (pre * gate).astype(BF16)
        hidden[at, :] = hid
        outer = dot(hid, wo_ref[...])
        centered = outer - row_mean(outer)
        inv_std = lax.rsqrt(row_mean(centered * centered) + norm_eps)
        normed = centered * inv_std
        gain = gain_ref[...]
        out_new[at, :] = (nf_ref[at, :].astype(F32) + normed * gain).astype(BF16)
        upstream = cot_ref[at, :].astype(F32)
        gained = upstream * gain
        back = ((gained - row_mean(gained) - normed * row_mean(gained * normed)) * inv_std).astype(BF16)
        outer_grad[at, :] = back
        back = (dot_right_t(back, wo_ref[...]) * (gate * (1.0 + pre * (1.0 - gate)))).astype(BF16)
        pre_grad[at, :] = back
        base[at, :] = upstream + dot_right_t(back, wi_ref[0:256, :])
        agg_grad[pl.ds(2 * c, 2)] = dot_right_t(back, wi_ref[256:512, :]).astype(BF16).reshape(2, 128, 256)
        return (
            sums[0] + jnp.sum(back.astype(F32), axis=0, keepdims=True),
            sums[1] + jnp.sum(upstream * normed, axis=0, keepdims=True),
        )

    zero_row = jnp.zeros((1, 256), F32)
    bias_sum, gain_sum = lax.fori_loop(0, node_rows // 256, node_update, (zero_row, zero_row))

    def deal(stage, first, tall, value):
        for rep in range(reps):
            for tile in range(8):
                start, half = (64 * rep + 16 * (tile // 2)) * tall, 128 * (tile % 2)
                slot, place = rep * plane + tile // sub, stage.shape[1] // sub * (tile % sub)
                stage[slot, place + first : place + first + 16 * tall, :] = value[
                    start : start + 16 * tall, half : half + 128
                ].astype(BF16)

    deal(stage_e, 0, 1, inner_rows(hidden[...], outer_grad[...]))
    back_all = pre_grad[...]
    deal(
        stage_e, 16, 2,
        jnp.concatenate([inner_rows(nf_ref[...], back_all), inner_rows(agg[...], back_all)], axis=0),
    )
    low_lane = lax.broadcasted_iota(jnp.int32, (1, 128), 1) < 64
    for rep in range(reps):
        at = slice(128 * (rep // 2), 128 * (rep // 2) + 128)
        left, right = bias_sum[:, at], gain_sum[:, at]
        if rep % 2:
            left = pltpu.roll(left, 64, 1)
        else:
            right = pltpu.roll(right, 64, 1)
        both = jnp.broadcast_to(jnp.where(low_lane, left, right), (16, 128)).astype(BF16)
        for g in range(plane):
            stage_e[rep * plane + g, 48:64, :] = both
    land_e[team_at] = stage_e[team_at]

    @pl.loop(1, team)
    def _(step):
        other, device = mate(step)
        send(stage_e.at[other], land_e.at[team_at], 1, device)

    def backward_slots(c, total):
        for lap in range(4):
            i = c * 4 + lap
            product = inner_rows(adj_ref[meta_s[4, i]], agg_grad[meta_s[5, i]])
            total = product + total * meta_s[6, i].astype(F32)
            run[i] = total
        return total

    carried = lax.fori_loop(0, 4, backward_slots, jnp.zeros((128, 256), F32))

    @pl.loop(0, peers)
    def _(k):
        at = pl.ds(pl.multiple_of(node_rows + k * 128, 128), 128)
        back = (run[meta_s[7, k]] * slope[at, :]).astype(BF16)
        halo_grad[pl.ds(pl.multiple_of(k * 128, 128), 128), :] = back
        rout[k] = dot_right_t(back, wm_ref[...]).astype(BF16)

    rin[2 + rep_at] = rout[2 + rep_at]
    send(rout.at[0], rin.at[0], 2, loop_down)
    send(rout.at[1], rin.at[1], 2, loop_up)

    @pl.loop(1, reps)
    def _(step):
        r_to = lax.rem(rep_at + step, reps)
        send(rout.at[2 + r_to], rin.at[2 + rep_at], 2, {"loop": loop_at, "rep": r_to})

    lax.fori_loop(4, 6, backward_slots, carried)

    @pl.loop(0, blocks)
    def _(b):
        at = pl.ds(pl.multiple_of(b * 128, 128), 128)
        own_grad[at, :] = (run[meta_s[7, peers + b]] * slope[at, :]).astype(BF16)

    message_grad = inner_rows(nf_ref[...], own_grad[...])
    for k in range(peers):
        message_grad += inner_rows(hin[k], halo_grad[128 * k : 128 * k + 128, :])
    deal(stage_l, 0, 1, message_grad)
    land_l[team_at] = stage_l[team_at]

    @pl.loop(1, team)
    def _(step):
        other, device = mate(step)
        send(stage_l.at[other], land_l.at[team_at], 3, device)

    @pl.loop(0, node_rows // 256)
    def _(c):
        at = pl.ds(pl.multiple_of(c * 256, 256), 256)
        base[at, :] += dot_right_t(own_grad[at, :], wm_ref[...])

    copy_all(rin.at[1:], recv_sem.at[2]).wait()
    copy_all(rin.at[1:], send_sem.at[2]).wait()

    @pl.loop(0, node_rows // 256)
    def _(c):
        at = pl.ds(pl.multiple_of(c * 256, 256), 256)
        total = base[at, :]
        for k in range(peers):
            total += dot(spread[at, 128 * k : 128 * k + 128], rin[k])
        out_grad[at, :] = total.astype(BF16)

    copy_all(land_e.at[1:], recv_sem.at[1]).wait()
    copy_all(land_l.at[1:], recv_sem.at[3]).wait()
    total_e = lax.fori_loop(
        1, team, lambda slot, total: total + land_e[slot].astype(F32), land_e[0].astype(F32)
    )
    total_l = lax.fori_loop(
        1, team, lambda slot, total: total + land_l[slot].astype(F32), land_l[0].astype(F32)
    )
    parts = []
    for tile in range(sub):
        parts += [total_e[64 * tile : 64 * tile + 48], total_l[16 * tile : 16 * tile + 16]]
    total = jnp.concatenate(parts, axis=0)
    vec_row = total_e[48:49]
    rows = 64 * sub // depth
    for z in range(depth):
        zsend[z, 0:rows, :] = total[z * rows : (z + 1) * rows]
        zsend[z, rows : rows + 1, :] = vec_row
        zsend[z, rows + 1 :, :] = jnp.zeros((zsend.shape[1] - rows - 1, 128), F32)
    zland[z_at] = zsend[z_at]

    @pl.loop(1, depth)
    def _(step):
        z_to, device = above(step)
        send(zsend.at[z_to], zland.at[z_at], 4, device)

    copy_all(zland.at[1:], recv_sem.at[4]).wait()
    total = zland[0]
    for z in range(1, depth):
        total = total + zland[z]
    total = total * scale
    out_vec[...] = total[rows : rows + 1]
    zpiece[...] = total[0:rows]
    zgather[z_at] = total[0:rows]

    @pl.loop(1, depth)
    def _(step):
        send(zpiece, zgather.at[z_at], 5, above(step)[1])

    copy_all(zgather.at[1:], recv_sem.at[5]).wait()
    piece = jnp.concatenate([zgather[z] for z in range(depth)], axis=0).astype(BF16)
    gpiece[...] = piece
    gather[g_at] = piece

    @pl.loop(1, plane)
    def _(step):
        g_to = lax.rem(g_at + step, plane)
        send(gpiece, gather.at[g_at], 6, {"loop": z_at * plane + g_to, "rep": rep_at})

    copy_all(gather.at[1:], recv_sem.at[6]).wait()
    for tile in range(8):
        row, half = 16 * (tile // 2), 128 * (tile % 2)
        slot, place = tile // sub, 64 * (tile % sub)
        for first, out, tall in ((0, out_ow, 1), (16, out_iw, 2), (48, out_mw, 1)):
            block = gather[slot, place + first : place + first + 16 * tall, :]
            out[row * tall : (row + 16) * tall, half : half + 128] = block.astype(F32)

    for sem, sent in ((1, land_e), (3, land_l), (4, zland), (5, zgather), (6, gather)):
        copy_all(sent.at[1:], send_sem.at[sem]).wait()


def shards(
    node_features,
    cotangent,
    adjacency,
    block_index,
    block_count,
    send_rows,
    row_counts,
    message_weight,
    input_weight,
    input_bias,
    output_weight,
    norm_gain,
):
    loop_size, reps = lax.axis_size("loop"), lax.axis_size("rep")
    plane, depth = plane_of(loop_size)
    sub = 8 // plane
    peers = 2 + reps
    node_rows, width = node_features.shape
    slots = adjacency.shape[2]
    rows = 64 * sub // depth
    zrows = -(-(rows + 1) // 8) * 8
    scale = 1.0 / math.sqrt(node_rows * loop_size * reps)
    vmem, smem = pl.BlockSpec(memory_space=pltpu.VMEM), pl.BlockSpec(memory_space=pltpu.SMEM)
    shape = jax.ShapeDtypeStruct
    table_rows = node_rows + peers * 128
    halo = pltpu.VMEM((peers, 128, width), BF16)
    wide = pltpu.VMEM((node_rows, width), BF16)
    outs = pl.pallas_call(
        functools.partial(layer_kernel, plane, depth, reps, scale),
        out_shape=(
            shape((node_rows, width), BF16),
            shape((node_rows, width), BF16),
            shape((width // reps, width), F32),
            shape((2 * width // reps, width), F32),
            shape((width // reps, width), F32),
            shape((1, 128), F32),
        ),
        in_specs=[vmem, vmem, vmem, vmem, smem, vmem, smem, vmem, vmem, vmem, vmem, vmem],
        out_specs=[vmem] * 6,
        scratch_shapes=[
            pltpu.VMEM((128, 128), jnp.int32),
            pltpu.VMEM((8, 128), jnp.int32),
            pltpu.SMEM((8, 128), jnp.int32),
            halo, halo, halo, halo,
            pltpu.VMEM((node_rows, peers * 128), BF16),
            pltpu.VMEM((table_rows // 128, 128, width), BF16),
            pltpu.VMEM((table_rows, width), F32),
            pltpu.VMEM((node_rows, width), F32),
            pltpu.VMEM((slots, 128, width), F32),
            wide, wide, wide, wide,
            pltpu.VMEM((node_rows // 128, 128, width), BF16),
            pltpu.VMEM((node_rows, width), F32),
            wide,
            pltpu.VMEM((peers * 128, width), BF16),
            pltpu.VMEM((reps * plane, 64 * sub, 128), BF16),
            pltpu.VMEM((reps * plane, 64 * sub, 128), BF16),
            pltpu.VMEM((reps * plane, 16 * sub, 128), BF16),
            pltpu.VMEM((reps * plane, 16 * sub, 128), BF16),
            pltpu.VMEM((depth, zrows, 128), F32),
            pltpu.VMEM((depth, zrows, 128), F32),
            pltpu.VMEM((rows, 128), F32),
            pltpu.VMEM((depth, rows, 128), F32),
            pltpu.VMEM((64 * sub, 128), BF16),
            pltpu.VMEM((plane, 64 * sub, 128), BF16),
            pltpu.SemaphoreType.DMA,
            pltpu.SemaphoreType.DMA((7,)),
            pltpu.SemaphoreType.DMA((7,)),
        ],
        compiler_params=pltpu.CompilerParams(
            collective_id=0, has_side_effects=True, vmem_limit_bytes=48 * 1024 * 1024
        ),
        name="message_layer",
    )(
        node_features,
        cotangent,
        adjacency[0, 0],
        block_index[0, 0],
        block_count,
        send_rows[0, 0],
        row_counts[0],
        message_weight,
        input_weight,
        input_bias[None, :],
        output_weight,
        norm_gain[None, :],
    )
    new_features, grad_features, grad_mw, grad_iw, grad_ow, vec = outs
    half = width // reps
    return new_features, grad_features, grad_mw, grad_iw, vec[0, :half], grad_ow, vec[0, half:]


def solution(mesh):
    in_specs = (
        P(("loop", "rep"), None),
        P(("loop", "rep"), None),
        P("loop", "rep", None, None, None),
        P("loop", "rep", None, None),
        P("loop", "rep"),
        P("loop", "rep", None, None),
        P("loop", "rep", None),
        P(),
        P(),
        P(),
        P(),
        P(),
    )
    out_specs = (
        P(("loop", "rep"), None),
        P(("loop", "rep"), None),
        P("rep", None),
        P("rep", None),
        P("rep"),
        P("rep", None),
        P("rep"),
    )
    return jax.shard_map(shards, mesh=mesh, in_specs=in_specs, out_specs=out_specs, check_vma=False)
```

time: 586 us -> 78.4 us (0.13)
  waiting for transfers between devices: 360 us -> 0 us
  blocking collectives: 99 us -> 0 us
  Pallas kernels: 0 us -> 64.8 us
  starting transfers between devices: 38.2 us -> 0 us
  matrix products: 26.6 us -> 0 us
  other arithmetic: 19.9 us -> 0 us
  local copies, waits for them, and re-layouts: 26.8 us -> 10.8 us
  between operations: 15.1 us -> 1.35 us
    psum x1 -> x0, waiting for transfers between devices: 356 us -> none  [shards(): lax.psum((partials[0], partials[1], partials[2], partials[3], partials[4]...]
    psum x1 -> x0, blocking collectives: 99 us -> none  [shards(): lax.psum((partials[0], partials[1], partials[2], partials[3], partials[4]...]
    pallas_call x0 -> x1, Pallas kernels: none -> 64.8 us  [shards(): pl.pallas_call(functools.partial(layer_kernel, plane, depth, reps, scale)...]
    dot_general x13 -> x0, matrix products: 26.6 us -> none  [the longest x3 5.72 us: inner_rows(): lax.dot_general(left_side, right_side, (((0,), (0,)), ((), ())), preferre...]
    ppermute x4 -> x0, starting transfers between devices: 23.6 us -> none  [shifted(): lax.ppermute(shard, axis, [(i, (i + by) % size) for i in range(size)])]
    all_to_all x2 -> x0, starting transfers between devices: 14.6 us -> none  [the longest x1 10.3 us: shards(): lax.all_to_all(outgoing[2:], 'rep', split_axis=0, concat_axis=0, tiled=True)]
    scatter-add x1 -> x0, other arithmetic: 6.63 us -> none  [shards(): own_part.at[row_lists.reshape(-1)].add(returned.reshape(-1, feat_width))]
    gather x3 -> x0, local copies, waits for them, and re-layouts: 6.37 us -> none  [the longest x1 2.65 us: shards(): jnp.take(message, row_lists.reshape(-1), axis=0)]
  transfers between devices with their start and end apart: 7 -> 0, of which waited for: 2 -> 0; matrix products, arithmetic and copies ran while one was open for 3% -> 0% of each run, Pallas kernels for 0% -> 0%
where the time goes in v2:
time: 78.4 us; the launch traced here: 77 us
  Pallas kernels  64.8 us (83%)
  local copies, waits for them, and re-layouts  10.8 us (14%)
  between operations  1.35 us (2%)
    pallas_call x1, Pallas kernels, shards(): pl.pallas_call(functools.partial(layer_kernel, plane, depth, reps, scale)...  64.8 us
    unnamed x28, local copies, waits for them, and re-layouts  10.2 us

profile of v2, /device:TPU:1, one launch (start us, length us, event | category | flops | bytes accessed | tf_op | source)
XLA Modules:
  0.0 77.0 jit_solution(13755484009505373106)
XLA Ops:
  0.6 0.0 copy-start.10
  1.3 0.0 copy-done.10
  1.3 0.0 copy-start.7
  1.3 0.0 copy-start.8
  1.3 0.0 copy-start.6
  1.4 0.0 copy-start.9
  1.4 0.6 copy-done.7
  2.0 0.0 copy-done.8
  2.0 0.0 copy-done.6
  2.0 0.0 copy-done.9
  2.0 0.0 copy-start
  2.0 1.1 %copy-done = bf16[1,1,24,128,128]{4,3,2,1,0:T(8,128)(2,1)S(1)} copy-done((bf16[1,1,24,128,128]{4,3,2,1,0:T(8,128)(2,1)S(1)}, bf16[1,1,24,128,128]{4,3,2,1,0:T(8,128)(2,1)}, u32[]{:S(2)}) %copy-start) | copy-done | bytes 786456
  3.2 0.0 copy-start.1
  3.2 1.0 %copy-done.1 = bf16[1024,256]{1,0:T(8,128)(2,1)S(1)} copy-done((bf16[1024,256]{1,0:T(8,128)(2,1)S(1)}, bf16[1024,256]{1,0:T(8,128)(2,1)}, u32[]{:S(2)}) %copy-start.1) | copy-done | bytes 524312
  4.2 0.0 copy-start.2
  4.2 1.0 %copy-done.2 = bf16[1024,256]{1,0:T(8,128)(2,1)S(1)} copy-done((bf16[1024,256]{1,0:T(8,128)(2,1)S(1)}, bf16[1024,256]{1,0:T(8,128)(2,1)}, u32[]{:S(2)}) %copy-start.2) | copy-done | bytes 524312
  5.3 0.0 copy-start.3
  5.3 0.9 %copy-done.3 = bf16[512,256]{1,0:T(8,128)(2,1)S(1)} copy-done((bf16[512,256]{1,0:T(8,128)(2,1)S(1)}, bf16[512,256]{1,0:T(8,128)(2,1)}, u32[]{:S(2)}) %copy-start.3) | copy-done | bytes 262168
  6.2 0.0 copy-start.4
  6.2 0.9 %copy-done.4 = bf16[256,256]{1,0:T(8,128)(2,1)S(1)} copy-done((bf16[256,256]{1,0:T(8,128)(2,1)S(1)}, bf16[256,256]{1,0:T(8,128)(2,1)}, u32[]{:S(2)}) %copy-start.4) | copy-done | bytes 131096
  7.1 0.0 copy-start.5
  7.1 0.9 %copy-done.5 = bf16[256,256]{1,0:T(8,128)(2,1)S(1)} copy-done((bf16[256,256]{1,0:T(8,128)(2,1)S(1)}, bf16[256,256]{1,0:T(8,128)(2,1)}, u32[]{:S(2)}) %copy-start.5) | copy-done | bytes 131096
  8.0 64.8 %message_layer.1 = (bf16[1024,256]{1,0:T(8,128)(2,1)S(1)}, bf16[1024,256]{1,0:T(8,128)(2,1)S(1)}, f32[64,256]{1,0:T(8,128)S(1)}, f32[128,256]{1,0:T(8,128)S(1)},...) custom-call(bf16[1024,256]{1,0:T(8,128)(2,1)S(1)} %copy-done.1, bf16[1024,256]{1,0:T(8,128)(2,1)S(1)} %copy-done.2, ...), custom_call_target="tpu_custom_call" | custom-call | tf_op jit(solution)/shard_map/message_layer/pallas_call | solution.py:406
  72.9 0.6 slice_bitcast_fusion
  73.5 0.8 %copy.28 = bf16[1024,256]{1,0:T(8,128)(2,1)} copy(bf16[1024,256]{1,0:T(8,128)(2,1)S(1)} %get-tuple-element.28) | data formatting | bytes 1048576
  74.3 0.8 %copy.29 = bf16[1024,256]{1,0:T(8,128)(2,1)} copy(bf16[1024,256]{1,0:T(8,128)(2,1)S(1)} %get-tuple-element.29) | data formatting | bytes 1048576
  75.0 0.6 copy.30
  75.7 0.7 copy.31
  76.3 0.6 copy.32
  (1 shorter events, 0.0 us)
Async XLA Ops:
  0.6 0.7 copy-start.10
  1.3 0.7 copy-start.7
  1.3 0.7 copy-start.8
  1.3 0.7 copy-start.6
  1.4 0.7 copy-start.9
  2.0 1.1 %copy-start = (bf16[1,1,24,128,128]{4,3,2,1,0:T(8,128)(2,1)S(1)}, bf16[1,1,24,128,128]{4,3,2,1,0:T(8,128)(2,1)}, u32[]{:S(2)}) copy-start(bf16[1,1,24,128,128]{4,3,2,1,0:T(8,128)(2,1)} %param.14) | copy-start | bytes 2359300
  3.2 1.0 %copy-start.1 = (bf16[1024,256]{1,0:T(8,128)(2,1)S(1)}, bf16[1024,256]{1,0:T(8,128)(2,1)}, u32[]{:S(2)}) copy-start(bf16[1024,256]{1,0:T(8,128)(2,1)} %nf_ref.1) | copy-start | bytes 1572868
  4.2 1.0 %copy-start.2 = (bf16[1024,256]{1,0:T(8,128)(2,1)S(1)}, bf16[1024,256]{1,0:T(8,128)(2,1)}, u32[]{:S(2)}) copy-start(bf16[1024,256]{1,0:T(8,128)(2,1)} %cot_ref.1) | copy-start | bytes 1572868
  5.3 0.9 %copy-start.3 = (bf16[512,256]{1,0:T(8,128)(2,1)S(1)}, bf16[512,256]{1,0:T(8,128)(2,1)}, u32[]{:S(2)}) copy-start(bf16[512,256]{1,0:T(8,128)(2,1)} %wi_ref.1) | copy-start | bytes 786436
  6.2 0.9 %copy-start.4 = (bf16[256,256]{1,0:T(8,128)(2,1)S(1)}, bf16[256,256]{1,0:T(8,128)(2,1)}, u32[]{:S(2)}) copy-start(bf16[256,256]{1,0:T(8,128)(2,1)} %wm_ref.1) | copy-start | bytes 393220
  7.1 0.9 %copy-start.5 = (bf16[256,256]{1,0:T(8,128)(2,1)S(1)}, bf16[256,256]{1,0:T(8,128)(2,1)}, u32[]{:S(2)}) copy-start(bf16[256,256]{1,0:T(8,128)(2,1)} %wo_ref.1) | copy-start | bytes 393220

commit v3 on v2

v3 whole, which is shorter than its diff:
```python
import functools
import math

import jax
import jax.numpy as jnp
from jax import lax
from jax.experimental import pallas as pl
from jax.experimental.pallas import tpu as pltpu
from jax.sharding import PartitionSpec as P

norm_eps = 1e-05
MESH = pl.DeviceIdType.MESH
BF16, F32 = jnp.bfloat16, jnp.float32


def dot(left, right):
    return jnp.dot(left, right, preferred_element_type=F32)


def dot_right_t(left, right):
    return lax.dot_general(left, right, (((1,), (1,)), ((), ())), preferred_element_type=F32)


def inner_rows(left, right):
    return lax.dot_general(left, right, (((0,), (0,)), ((), ())), preferred_element_type=F32)


def sigmoid(argument):
    return 0.5 * jnp.tanh(0.5 * argument) + 0.5


def row_mean(values):
    return jnp.sum(values, axis=-1, keepdims=True) * (1.0 / values.shape[-1])


def plane_of(loop_size):
    plane = 8 if loop_size % 8 == 0 and loop_size > 8 else 2
    return plane, loop_size // plane


def copy_all(buffer, sem):
    return pltpu.make_async_copy(buffer, buffer, sem)


def slot_order(key_col, key_row, cols):
    shape = (32, 128)
    slot = lax.broadcasted_iota(jnp.int32, shape, 0)
    lane = lax.broadcasted_iota(jnp.int32, shape, 1)
    ahead = (key_row < key_col) | ((key_row == key_col) & (lane < slot))
    rank = jnp.sum(jnp.where(ahead & (lane < 24), 1, 0), axis=1, keepdims=True)
    placed = (rank == lane) & (slot < 24)
    rows = [
        jnp.sum(jnp.where(placed, col, 0), axis=0, keepdims=True) for col in (slot, *cols, key_col)
    ]
    before = pltpu.roll(rows[-1], 1, 1)
    keep = jnp.where((rows[-1] == before) & (lane[:1] > 0), 1, 0)
    last = jnp.sum(jnp.where((key_col <= lane) & (slot < 24), 1, 0), axis=0, keepdims=True) - 1
    last = jnp.maximum(last, 0)
    return [*rows[:-1], keep, last]


def silu_and_slope(pre):
    gate = sigmoid(pre)
    return (pre * gate).astype(BF16), gate * (1.0 + pre * (1.0 - gate))


def remote(source, target, send_sem, recv_sem, device):
    pltpu.make_async_remote_copy(
        source, target, send_sem, recv_sem, device_id=device, device_id_type=MESH
    ).start()


def greet(device):
    pl.semaphore_signal(pltpu.get_barrier_semaphore(), inc=1, device_id=device, device_id_type=MESH)


def halo_kernel(
    reps, loop_size,
    nf_hbm, index_ref, count_ref, rows_ref, kept_ref,
    hin, meta,
    nf_ref, flat, hout, load_sem, send_sem, recv_sem,
):
    node_rows = nf_ref.shape[0]
    blocks = node_rows // 128
    peers = 2 + reps
    loop_at, rep_at = lax.axis_index("loop"), lax.axis_index("rep")
    loop_up = {"loop": lax.rem(loop_at + 1, loop_size), "rep": rep_at}
    loop_down = {"loop": lax.rem(loop_at + loop_size - 1, loop_size), "rep": rep_at}

    load = pltpu.make_async_copy(nf_hbm, nf_ref, load_sem)
    load.start()
    greet(loop_up)
    greet(loop_down)
    for step in range(1, reps):
        greet({"loop": loop_at, "rep": lax.rem(rep_at + step, reps)})
    flat[...] = jnp.zeros(flat.shape, jnp.int32)
    flat[0:2, 0:24] = index_ref[...]
    for k in range(peers):
        flat[8 + k : 9 + k, :] = rows_ref[k]
    turned = jnp.transpose(flat[...])
    lane_rows = lax.broadcasted_iota(jnp.int32, (128, node_rows), 1)
    sub_rows = lax.broadcasted_iota(jnp.int32, (128, node_rows), 0)
    load.wait()
    for k in range(peers):
        live = (lane_rows == turned[:, 8 + k : 9 + k]) & (sub_rows < kept_ref[0, k])
        picker = jnp.where(live, 1.0, 0.0).astype(BF16)
        hout[k] = dot(picker, nf_ref[...]).astype(BF16)

    pl.semaphore_wait(pltpu.get_barrier_semaphore(), 1 + reps)
    remote(hout.at[0], hin.at[0], send_sem, recv_sem, loop_up)
    remote(hout.at[1], hin.at[1], send_sem, recv_sem, loop_down)
    for step in range(1, reps):
        r_to = lax.rem(rep_at + step, reps)
        remote(
            hout.at[2 + r_to], hin.at[2 + rep_at], send_sem, recv_sem, {"loop": loop_at, "rep": r_to}
        )
    own = pltpu.make_async_copy(hout.at[2 + rep_at], hin.at[2 + rep_at], load_sem)
    own.start()

    live_total = count_ref[0, 0]
    slot_col = lax.broadcasted_iota(jnp.int32, (32, 1), 0)
    slot_row = lax.broadcasted_iota(jnp.int32, (1, 128), 1)
    dest_col, source_col = turned[0:32, 0:1], turned[0:32, 1:2]
    dest_row, source_row = flat[0:1, :], flat[1:2, :]

    def keyed(value, iota):
        return jnp.where(iota < live_total, value, 64)

    def halo_first(value):
        return jnp.where(value >= blocks, value - blocks, value + peers)

    forward = slot_order(keyed(dest_col, slot_col), keyed(dest_row, slot_row), (source_col,))
    backward = slot_order(
        keyed(halo_first(source_col), slot_col), keyed(halo_first(source_row), slot_row), (dest_col,)
    )
    meta[...] = jnp.concatenate(forward + backward, axis=0)

    own.wait()
    copy_all(hin.at[1:], recv_sem).wait()
    copy_all(hin.at[1:], send_sem).wait()


def layer_kernel(
    plane, depth, reps, scale,
    nf_hbm, wm_hbm, hin_hbm, wi_hbm, meta_hbm, adj_hbm, cot_hbm, wo_hbm,
    rows_ref, kept_ref, bias_ref, gain_ref,
    new_hbm, grad_hbm, mw_hbm, iw_hbm, grad_bias_hbm, ow_hbm, grad_gain_hbm,
    nf_ref, wm_ref, hin, wi_ref, meta_s, adj_ref, cot_ref, wo_ref,
    out_new, out_grad, out_mw, out_iw, out_bias, out_ow, out_gain,
    rout, rin, table, own_slope, halo_slope, pre_part, spread, run,
    agg, hidden, outer_grad, pre_grad, agg_grad, base, own_grad, halo_grad,
    stage_e, land_e, zsend, zland, zpiece, zgather, gpiece_e, gather_e,
    stage_l, land_l, lpiece, lland, gpiece_l, gather_l,
    load_sem, store_sem, send_sem, recv_sem,
):
    sub = 8 // plane
    node_rows = nf_ref.shape[0]
    blocks = node_rows // 128
    peers = 2 + reps
    loop_size = plane * depth
    loop_at, rep_at = lax.axis_index("loop"), lax.axis_index("rep")
    z_at, g_at = loop_at // plane, lax.rem(loop_at, plane)
    team = reps * plane
    team_at = rep_at * plane + g_at
    loop_up = {"loop": lax.rem(loop_at + 1, loop_size), "rep": rep_at}
    loop_down = {"loop": lax.rem(loop_at + loop_size - 1, loop_size), "rep": rep_at}

    def mate(step):
        other = lax.rem(team_at + step, team)
        r_to, g_to = other // plane, lax.rem(other, plane)
        return other, {"loop": z_at * plane + g_to, "rep": r_to}

    def above(step):
        z_to = lax.rem(z_at + step, depth)
        return z_to, {"loop": z_to * plane + g_at, "rep": rep_at}

    def send(source, target, sem, device):
        remote(source, target, send_sem.at[sem], recv_sem.at[sem], device)

    def to_team(stage, land, sem):
        land[team_at] = stage[team_at]

        @pl.loop(1, team)
        def _(step):
            other, device = mate(step)
            send(stage.at[other], land.at[team_at], sem, device)

    def to_plane(piece, gather, sem):
        gather[g_at] = piece[...]

        @pl.loop(1, plane)
        def _(step):
            g_to = lax.rem(g_at + step, plane)
            send(piece, gather.at[g_at], sem, {"loop": z_at * plane + g_to, "rep": rep_at})

    def arrived(land, sem):
        copy_all(land.at[1:], recv_sem.at[sem]).wait()

    def added(land, count):
        total = land[0].astype(F32)
        return lax.fori_loop(1, count, lambda slot, total: total + land[slot].astype(F32), total)

    loads = [
        pltpu.make_async_copy(source, target, load_sem.at[i])
        for i, (source, target) in enumerate(
            (
                (nf_hbm, nf_ref), (wm_hbm, wm_ref), (hin_hbm, hin), (wi_hbm, wi_ref),
                (meta_hbm, meta_s), (adj_hbm, adj_ref), (cot_hbm, cot_ref), (wo_hbm, wo_ref),
            )
        )
    ]
    for load in loads:
        load.start()
    stores = [
        pltpu.make_async_copy(source, target, store_sem.at[i])
        for i, (source, target) in enumerate(
            (
                (out_new, new_hbm), (out_grad, grad_hbm), (out_mw, mw_hbm), (out_iw, iw_hbm),
                (out_bias, grad_bias_hbm), (out_ow, ow_hbm), (out_gain, grad_gain_hbm),
            )
        )
    ]

    @pl.loop(1, depth)
    def _(step):
        greet(above(step)[1])

    @pl.loop(1, team)
    def _(step):
        greet(mate(step)[1])

    greet(loop_up)
    greet(loop_down)

    for load in loads[:4]:
        load.wait()

    @pl.loop(0, node_rows // 256)
    def _(c):
        at = pl.ds(pl.multiple_of(c * 256, 256), 256)
        features = nf_ref[at, :]
        message, own_slope[at, :] = silu_and_slope(dot(features, wm_ref[...]))
        table[pl.ds(2 * c, 2)] = message.reshape(2, 128, 256)
        pre_part[at, :] = dot(features, wi_ref[0:256, :]) + bias_ref[...]

    @pl.loop(0, peers)
    def _(k):
        table[blocks + k], halo_slope[k] = silu_and_slope(dot(hin[k], wm_ref[...]))

    for load in loads[4:]:
        load.wait()

    def forward_slots(c, total):
        for lap in range(4):
            i = c * 4 + lap
            product = dot(adj_ref[meta_s[0, i]], table[meta_s[1, i]])
            total = product + total * meta_s[2, i].astype(F32)
            run[i] = total
        return total

    lax.fori_loop(0, 6, forward_slots, jnp.zeros((128, 256), F32))

    def node_update(c, sums):
        at = pl.ds(pl.multiple_of(c * 256, 256), 256)
        gathered = jnp.concatenate(
            [run[meta_s[3, 2 * c]], run[meta_s[3, 2 * c + 1]]], axis=0
        ).astype(BF16)
        agg[at, :] = gathered
        hid, hid_slope = silu_and_slope(pre_part[at, :] + dot(gathered, wi_ref[256:512, :]))
        hidden[at, :] = hid
        outer = dot(hid, wo_ref[...])
        centered = outer - row_mean(outer)
        inv_std = lax.rsqrt(row_mean(centered * centered) + norm_eps)
        normed = centered * inv_std
        gain = gain_ref[...]
        out_new[at, :] = (nf_ref[at, :].astype(F32) + normed * gain).astype(BF16)
        upstream = cot_ref[at, :].astype(F32)
        gained = upstream * gain
        back = ((gained - row_mean(gained) - normed * row_mean(gained * normed)) * inv_std).astype(BF16)
        outer_grad[at, :] = back
        back = (dot_right_t(back, wo_ref[...]) * hid_slope).astype(BF16)
        pre_grad[at, :] = back
        base[at, :] = upstream + dot_right_t(back, wi_ref[0:256, :])
        agg_grad[pl.ds(2 * c, 2)] = dot_right_t(back, wi_ref[256:512, :]).astype(BF16).reshape(2, 128, 256)
        return (
            sums[0] + jnp.sum(back.astype(F32), axis=0, keepdims=True),
            sums[1] + jnp.sum(upstream * normed, axis=0, keepdims=True),
        )

    zero_row = jnp.zeros((1, 256), F32)
    bias_sum, gain_sum = lax.fori_loop(0, node_rows // 256, node_update, (zero_row, zero_row))

    stores[0].start()

    def deal(stage, first, tall, value):
        for rep in range(reps):
            for tile in range(8):
                start, half = (64 * rep + 16 * (tile // 2)) * tall, 128 * (tile % 2)
                slot, place = rep * plane + tile // sub, stage.shape[1] // sub * (tile % sub)
                stage[slot, place + first : place + first + 16 * tall, :] = value[
                    start : start + 16 * tall, half : half + 128
                ].astype(BF16)

    deal(stage_e, 0, 1, inner_rows(hidden[...], outer_grad[...]))
    back_all = pre_grad[...]
    deal(
        stage_e, 16, 2,
        jnp.concatenate([inner_rows(nf_ref[...], back_all), inner_rows(agg[...], back_all)], axis=0),
    )
    low_lane = lax.broadcasted_iota(jnp.int32, (1, 128), 1) < 64
    for rep in range(reps):
        at = slice(128 * (rep // 2), 128 * (rep // 2) + 128)
        left, right = bias_sum[:, at], gain_sum[:, at]
        if rep % 2:
            left = pltpu.roll(left, 64, 1)
        else:
            right = pltpu.roll(right, 64, 1)
        both = jnp.broadcast_to(jnp.where(low_lane, left, right), (16, 128)).astype(BF16)
        for g in range(plane):
            stage_e[rep * plane + g, 48:64, :] = both

    pl.semaphore_wait(pltpu.get_barrier_semaphore(), team + depth)
    to_team(stage_e, land_e, 0)

    def backward_slots(c, total):
        for lap in range(4):
            i = c * 4 + lap
            product = inner_rows(adj_ref[meta_s[4, i]], agg_grad[meta_s[5, i]])
            total = product + total * meta_s[6, i].astype(F32)
            run[i] = total
        return total

    carried = lax.fori_loop(0, 4, backward_slots, jnp.zeros((128, 256), F32))

    @pl.loop(0, peers)
    def _(k):
        back = (run[meta_s[7, k]] * halo_slope[k]).astype(BF16)
        halo_grad[k] = back
        rout[k] = dot_right_t(back, wm_ref[...]).astype(BF16)

    rin[2 + rep_at] = rout[2 + rep_at]
    send(rout.at[0], rin.at[0], 1, loop_down)
    send(rout.at[1], rin.at[1], 1, loop_up)
    for step in range(1, reps):
        r_to = lax.rem(rep_at + step, reps)
        send(rout.at[2 + r_to], rin.at[2 + rep_at], 1, {"loop": loop_at, "rep": r_to})

    lax.fori_loop(4, 6, backward_slots, carried)

    @pl.loop(0, blocks)
    def _(b):
        at = pl.ds(pl.multiple_of(b * 128, 128), 128)
        own_grad[at, :] = (run[meta_s[7, peers + b]] * own_slope[at, :]).astype(BF16)

    message_grad = inner_rows(nf_ref[...], own_grad[...])
    for k in range(peers):
        message_grad += inner_rows(hin[k], halo_grad[k])
    deal(stage_l, 0, 1, message_grad)
    to_team(stage_l, land_l, 2)

    @pl.loop(0, node_rows // 256)
    def _(c):
        at = pl.ds(pl.multiple_of(c * 256, 256), 256)
        base[at, :] += dot_right_t(own_grad[at, :], wm_ref[...])

    row_at = lax.broadcasted_iota(jnp.int32, (node_rows, 128), 0)
    lane_at = lax.broadcasted_iota(jnp.int32, (node_rows, 128), 1)
    for k in range(peers):
        live = (row_at == rows_ref[k]) & (lane_at < kept_ref[0, k])
        spread[:, 128 * k : 128 * k + 128] = jnp.where(live, 1.0, 0.0).astype(BF16)

    arrived(land_e, 0)
    total = added(land_e, team)
    vec_row = total[48:49]
    total = jnp.concatenate([total[64 * tile : 64 * tile + 48] for tile in range(sub)], axis=0)
    rows = 48 * sub // depth
    for z in range(depth):
        zsend[z, 0:rows, :] = total[z * rows : (z + 1) * rows]
        zsend[z, rows : rows + 1, :] = vec_row
    zland[z_at] = zsend[z_at]

    @pl.loop(1, depth)
    def _(step):
        z_to, device = above(step)
        send(zsend.at[z_to], zland.at[z_at], 3, device)

    arrived(land_l, 2)
    lpiece[...] = added(land_l, team).astype(BF16)
    lland[z_at] = lpiece[...]

    @pl.loop(1, depth)
    def _(step):
        send(lpiece, lland.at[z_at], 4, above(step)[1])

    arrived(rin, 1)

    @pl.loop(0, node_rows // 256)
    def _(c):
        at = pl.ds(pl.multiple_of(c * 256, 256), 256)
        total = base[at, :]
        for k in range(peers):
            total += dot(spread[at, 128 * k : 128 * k + 128], rin[k])
        out_grad[at, :] = total.astype(BF16)

    stores[1].start()
    arrived(zland, 3)
    total = added(zland, depth) * scale
    vec_row = total[rows : rows + 1]
    half = out_bias.shape[1]
    out_bias[...] = vec_row[:, 0:half]
    out_gain[...] = pltpu.roll(vec_row, half, 1)[:, 0:half]
    stores[4].start()
    stores[6].start()
    zpiece[...] = total
    zgather[z_at] = total

    @pl.loop(1, depth)
    def _(step):
        send(zpiece, zgather.at[z_at], 5, above(step)[1])

    arrived(lland, 4)
    gpiece_l[...] = (added(lland, depth) * scale).astype(BF16)
    to_plane(gpiece_l, gather_l, 6)

    arrived(zgather, 5)
    gpiece_e[...] = jnp.concatenate([zgather[z, 0:rows, :] for z in range(depth)], axis=0).astype(BF16)
    to_plane(gpiece_e, gather_e, 7)

    def collect(out, gather, first, tall):
        for tile in range(8):
            row, half = 16 * tall * (tile // 2), 128 * (tile % 2)
            slot, place = tile // sub, gather.shape[1] // sub * (tile % sub)
            block = gather[slot, place + first : place + first + 16 * tall, :]
            out[row : row + 16 * tall, half : half + 128] = block.astype(F32)

    arrived(gather_l, 6)
    collect(out_mw, gather_l, 0, 1)
    stores[2].start()
    arrived(gather_e, 7)
    collect(out_ow, gather_e, 0, 1)
    stores[5].start()
    collect(out_iw, gather_e, 16, 2)
    stores[3].start()

    sent = (land_e, rin, land_l, zland, lland, zgather, gather_l, gather_e)
    for sem, land in enumerate(sent):
        copy_all(land.at[1:], send_sem.at[sem]).wait()
    for store in stores:
        store.wait()


def finish_kernel(*refs):
    sem = refs[-1]
    copies = [
        pltpu.make_async_copy(source, target, sem.at[i])
        for i, (source, target) in enumerate(zip(refs[:7], refs[7:14]))
    ]
    for copy in copies:
        copy.start()
    for copy in copies:
        copy.wait()


def shards(
    node_features,
    cotangent,
    adjacency,
    block_index,
    block_count,
    send_rows,
    row_counts,
    message_weight,
    input_weight,
    input_bias,
    output_weight,
    norm_gain,
):
    loop_size, reps = lax.axis_size("loop"), lax.axis_size("rep")
    plane, depth = plane_of(loop_size)
    sub = 8 // plane
    peers = 2 + reps
    node_rows, width = node_features.shape
    blocks = node_rows // 128
    slots = adjacency.shape[2]
    rows = 48 * sub // depth + 1
    zrows = rows if rows <= 4 else -(-rows // 8) * 8
    scale = 1.0 / math.sqrt(node_rows * loop_size * reps)
    vmem, smem = pl.BlockSpec(memory_space=pltpu.VMEM), pl.BlockSpec(memory_space=pltpu.SMEM)
    hbm = pl.BlockSpec(memory_space=pltpu.HBM)
    shape = jax.ShapeDtypeStruct
    wide = (node_rows, width)
    mega = 1024 * 1024
    rows_in = send_rows.reshape(peers, 1, 128)
    hin, meta = pl.pallas_call(
        functools.partial(halo_kernel, reps, loop_size),
        out_shape=(shape((peers, 128, width), BF16), shape((8, 128), jnp.int32)),
        in_specs=[hbm, vmem, smem, vmem, smem],
        out_specs=[hbm, vmem],
        scratch_shapes=[
            pltpu.VMEM(wide, BF16),
            pltpu.VMEM((128, 128), jnp.int32),
            pltpu.VMEM((peers, 128, width), BF16),
            pltpu.SemaphoreType.DMA,
            pltpu.SemaphoreType.DMA,
            pltpu.SemaphoreType.DMA,
        ],
        compiler_params=pltpu.CompilerParams(
            collective_id=0, has_side_effects=True, vmem_limit_bytes=56 * mega
        ),
        name="halo_rows",
    )(node_features, block_index[0, 0], block_count, rows_in, row_counts[0])
    small = pltpu.VMEM(wide, BF16)
    half = width // reps
    results = (
        shape(wide, BF16),
        shape(wide, BF16),
        shape((half, width), F32),
        shape((2 * half, width), F32),
        shape((1, half), F32),
        shape((half, width), F32),
        shape((1, half), F32),
    )
    outs = pl.pallas_call(
        functools.partial(layer_kernel, plane, depth, reps, scale),
        out_shape=results,
        in_specs=[hbm] * 8 + [vmem, smem, vmem, vmem],
        out_specs=[hbm] * 7,
        scratch_shapes=[
            small,
            pltpu.VMEM((width, width), BF16),
            pltpu.VMEM((peers, 128, width), BF16),
            pltpu.VMEM((2 * width, width), BF16),
            pltpu.SMEM((8, 128), jnp.int32),
            pltpu.VMEM((slots, 128, 128), BF16),
            small,
            pltpu.VMEM((width, width), BF16),
            *(pltpu.VMEM(result.shape, result.dtype) for result in results),
            pltpu.VMEM((peers, 128, width), BF16),
            pltpu.VMEM((peers, 128, width), BF16),
            pltpu.VMEM((blocks + peers, 128, width), BF16),
            pltpu.VMEM(wide, F32),
            pltpu.VMEM((peers, 128, width), F32),
            pltpu.VMEM(wide, F32),
            pltpu.VMEM((node_rows, peers * 128), BF16),
            pltpu.VMEM((slots, 128, width), F32),
            small, small, small, small,
            pltpu.VMEM((blocks, 128, width), BF16),
            pltpu.VMEM(wide, F32),
            small,
            pltpu.VMEM((peers, 128, width), BF16),
            pltpu.VMEM((reps * plane, 64 * sub, 128), BF16),
            pltpu.VMEM((reps * plane, 64 * sub, 128), BF16),
            pltpu.VMEM((depth, zrows, 128), F32),
            pltpu.VMEM((depth, zrows, 128), F32),
            pltpu.VMEM((zrows, 128), F32),
            pltpu.VMEM((depth, zrows, 128), F32),
            pltpu.VMEM((48 * sub, 128), BF16),
            pltpu.VMEM((plane, 48 * sub, 128), BF16),
            pltpu.VMEM((reps * plane, 16 * sub, 128), BF16),
            pltpu.VMEM((reps * plane, 16 * sub, 128), BF16),
            pltpu.VMEM((16 * sub, 128), BF16),
            pltpu.VMEM((depth, 16 * sub, 128), BF16),
            pltpu.VMEM((16 * sub, 128), BF16),
            pltpu.VMEM((plane, 16 * sub, 128), BF16),
            pltpu.SemaphoreType.DMA((8,)),
            pltpu.SemaphoreType.DMA((7,)),
            pltpu.SemaphoreType.DMA((8,)),
            pltpu.SemaphoreType.DMA((8,)),
        ],
        compiler_params=pltpu.CompilerParams(
            collective_id=1, has_side_effects=True, vmem_limit_bytes=56 * mega
        ),
        name="message_layer",
    )(
        node_features,
        message_weight,
        hin,
        input_weight,
        meta,
        adjacency[0, 0],
        cotangent,
        output_weight,
        rows_in,
        row_counts[0],
        input_bias[None, :],
        norm_gain[None, :],
    )
    new_features, grad_features, grad_mw, grad_iw, grad_bias, grad_ow, grad_gain = pl.pallas_call(
        finish_kernel,
        out_shape=results,
        in_specs=[hbm] * 7,
        out_specs=[hbm] * 7,
        scratch_shapes=[pltpu.SemaphoreType.DMA((7,))],
        compiler_params=pltpu.CompilerParams(has_side_effects=True, vmem_limit_bytes=56 * mega),
        name="write_results",
    )(*outs)
    return (
        new_features, grad_features, grad_mw, grad_iw,
        grad_bias.reshape(half), grad_ow, grad_gain.reshape(half),
    )


def solution(mesh):
    in_specs = (
        P(("loop", "rep"), None),
        P(("loop", "rep"), None),
        P("loop", "rep", None, None, None),
        P("loop", "rep", None, None),
        P("loop", "rep"),
        P("loop", "rep", None, None),
        P("loop", "rep", None),
        P(),
        P(),
        P(),
        P(),
        P(),
    )
    out_specs = (
        P(("loop", "rep"), None),
        P(("loop", "rep"), None),
        P("rep", None),
        P("rep", None),
        P("rep"),
        P("rep", None),
        P("rep"),
    )
    return jax.shard_map(shards, mesh=mesh, in_specs=in_specs, out_specs=out_specs, check_vma=False)
```

time: 78.4 us -> 105 us (1.34)
  Pallas kernels: 64.8 us -> 102 us
  local copies, waits for them, and re-layouts: 10.8 us -> 0 us
    pallas_call x0 -> x2, Pallas kernels: none -> 62.4 us  [the longest x1 40.9 us: shards(): pl.pallas_call(finish_kernel, out_shape=results, in_specs=[hbm] * 7, out_...]
    pallas_call x1, Pallas kernels: 64.8 us -> 39.7 us  [shards(): pl.pallas_call(functools.partial(layer_kernel, plane, depth, reps, scale)...]
    unnamed x28 -> x0, local copies, waits for them, and re-layouts: 10.2 us -> none
where the time goes in v3:
time: 105 us; the launch traced here: 103 us
  Pallas kernels  102 us (97%)
  between operations  1.29 us (1%)
    pallas_call x1, Pallas kernels, shards(): pl.pallas_call(finish_kernel, out_shape=results, in_specs=[hbm] * 7, out_...  40.9 us
    pallas_call x1, Pallas kernels, shards(): pl.pallas_call(functools.partial(layer_kernel, plane, depth, reps, scale)...  39.7 us
    pallas_call x1, Pallas kernels, shards(): pl.pallas_call(functools.partial(halo_kernel, reps, loop_size), out_shape...  21.5 us

profile of v3, /device:TPU:1, one launch (start us, length us, event | category | flops | bytes accessed | tf_op | source)
XLA Modules:
  0.0 103.4 jit_solution(13161309202143269875)
XLA Ops:
  1.3 21.5 %halo_rows.1 = (bf16[6,128,256]{2,1,0:T(8,128)(2,1)}, s32[8,128]{1,0:T(8,128)}) custom-call(bf16[1024,256]{1,0:T(8,128)(2,1)} %nf_hbm.3, s32[2,24]{1,0:T(2,128)} %bitcast.13, s32[1,1]{1,0:T(1,128)S(6)} %copy.19.count_ref, s32[6,1,128]{2,1,0:T(1,128)} %bitcast.9, s32[1,6]{1,0:T(1,128)} %bitcast.11), custom_call_target="tpu_custom_call" | custom-call | tf_op jit(solution)/shard_map/halo_rows/pallas_call | solution.py:494
  22.8 39.7 %message_layer.1 = (bf16[1024,256]{1,0:T(8,128)(2,1)}, bf16[1024,256]{1,0:T(8,128)(2,1)}, f32[64,256]{1,0:T(8,128)}, f32[128,256]{1,0:T(8,128)}, f32[1,64]{1,0:T...) custom-call(bf16[1024,256]{1,0:T(8,128)(2,1)} %nf_hbm.3, bf16[256,256]{1,0:T(8,128)(2,1)} %wm_hbm.1, ...), custom_call_target="tpu_custom_call" | custom-call | tf_op jit(solution)/shard_map/message_layer/pallas_call | solution.py:523
  62.5 40.9 %write_results.1 = (bf16[1024,256]{1,0:T(8,128)(2,1)}, bf16[1024,256]{1,0:T(8,128)(2,1)}, f32[64,256]{1,0:T(8,128)}, f32[128,256]{1,0:T(8,128)}, f32[1,64]{1,0:T...) custom-call(bf16[1024,256]{1,0:T(8,128)(2,1)} %get-tuple-element.25.refs_0_, bf16[1024,256]{1,0:T(8,128)(2,1)} %get-tuple-element.26.refs_1_, ...), custom_call_target="tpu_custom_call" | custom-call | tf_op jit(solution)/shard_map/write_results/pallas_call | solution.py:588

commit v4 on v3

--- a/solution.py
+++ b/solution.py
@@ -101,14 +101,19 @@
     lane_rows = lax.broadcasted_iota(jnp.int32, (128, node_rows), 1)
     sub_rows = lax.broadcasted_iota(jnp.int32, (128, node_rows), 0)
     load.wait()
-    for k in range(peers):
+
+    def pick(k):
         live = (lane_rows == turned[:, 8 + k : 9 + k]) & (sub_rows < kept_ref[0, k])
         picker = jnp.where(live, 1.0, 0.0).astype(BF16)
         hout[k] = dot(picker, nf_ref[...]).astype(BF16)
 
+    pick(0)
+    pick(1)
     pl.semaphore_wait(pltpu.get_barrier_semaphore(), 1 + reps)
     remote(hout.at[0], hin.at[0], send_sem, recv_sem, loop_up)
     remote(hout.at[1], hin.at[1], send_sem, recv_sem, loop_down)
+    for k in range(2, peers):
+        pick(k)
     for step in range(1, reps):
         r_to = lax.rem(rep_at + step, reps)
         remote(
@@ -142,14 +147,14 @@
 
 def layer_kernel(
     plane, depth, reps, scale,
-    nf_hbm, wm_hbm, hin_hbm, wi_hbm, meta_hbm, adj_hbm, cot_hbm, wo_hbm,
+    nf_hbm, wm_hbm, wi_hbm, hin_hbm, meta_hbm, adj_hbm, cot_hbm, wo_hbm,
     rows_ref, kept_ref, bias_ref, gain_ref,
     new_hbm, grad_hbm, mw_hbm, iw_hbm, grad_bias_hbm, ow_hbm, grad_gain_hbm,
-    nf_ref, wm_ref, hin, wi_ref, meta_s, adj_ref, cot_ref, wo_ref,
+    nf_ref, wm_ref, wi_ref, hin, meta_s, adj_ref, cot_ref, wo_ref,
     out_new, out_grad, out_mw, out_iw, out_bias, out_ow, out_gain,
     rout, rin, table, own_slope, halo_slope, pre_part, spread, run,
     agg, hidden, outer_grad, pre_grad, agg_grad, base, own_grad, halo_grad,
-    stage_e, land_e, zsend, zland, zpiece, zgather, gpiece_e, gather_e,
+    stage_e, land_e, psend, pland, epiece, eland, gpiece_e, gather_e,
     stage_l, land_l, lpiece, lland, gpiece_l, gather_l,
     load_sem, store_sem, send_sem, recv_sem,
 ):
@@ -174,6 +179,14 @@
         z_to = lax.rem(z_at + step, depth)
         return z_to, {"loop": z_to * plane + g_at, "rep": rep_at}
 
+    parity = lax.rem(z_at, 2)
+    z_pair = z_at + 1 - 2 * parity
+
+    def twin(step):
+        other = lax.rem(parity * plane + g_at + step, 2 * plane)
+        z_to, g_to = z_at - parity + other // plane, lax.rem(other, plane)
+        return {"loop": z_to * plane + g_to, "rep": rep_at}
+
     def send(source, target, sem, device):
         remote(source, target, send_sem.at[sem], recv_sem.at[sem], device)
 
@@ -194,7 +207,8 @@
             send(piece, gather.at[g_at], sem, {"loop": z_at * plane + g_to, "rep": rep_at})
 
     def arrived(land, sem):
-        copy_all(land.at[1:], recv_sem.at[sem]).wait()
+        if land.shape[0] > 1:
+            copy_all(land.at[1:], recv_sem.at[sem]).wait()
 
     def added(land, count):
         total = land[0].astype(F32)
@@ -204,7 +218,7 @@
         pltpu.make_async_copy(source, target, load_sem.at[i])
         for i, (source, target) in enumerate(
             (
-                (nf_hbm, nf_ref), (wm_hbm, wm_ref), (hin_hbm, hin), (wi_hbm, wi_ref),
+                (nf_hbm, nf_ref), (wm_hbm, wm_ref), (wi_hbm, wi_ref), (hin_hbm, hin),
                 (meta_hbm, meta_s), (adj_hbm, adj_ref), (cot_hbm, cot_ref), (wo_hbm, wo_ref),
             )
         )
@@ -229,10 +243,14 @@
     def _(step):
         greet(mate(step)[1])
 
+    @pl.loop(1, plane)
+    def _(step):
+        greet({"loop": z_pair * plane + lax.rem(g_at + step, plane), "rep": rep_at})
+
     greet(loop_up)
     greet(loop_down)
 
-    for load in loads[:4]:
+    for load in loads[:3]:
         load.wait()
 
     @pl.loop(0, node_rows // 256)
@@ -243,12 +261,16 @@
         table[pl.ds(2 * c, 2)] = message.reshape(2, 128, 256)
         pre_part[at, :] = dot(features, wi_ref[0:256, :]) + bias_ref[...]
 
-    @pl.loop(0, peers)
-    def _(k):
-        table[blocks + k], halo_slope[k] = silu_and_slope(dot(hin[k], wm_ref[...]))
-
-    for load in loads[4:]:
-        load.wait()
+    loads[3].wait()
+    half_peers = peers // 2
+    for first in range(0, peers, half_peers):
+        some = slice(first, first + half_peers)
+        message, gate = silu_and_slope(dot(hin[some].reshape(half_peers * 128, 256), wm_ref[...]))
+        table[blocks + first : blocks + first + half_peers] = message.reshape(half_peers, 128, 256)
+        halo_slope[some] = gate.reshape(half_peers, 128, 256)
+
+    loads[4].wait()
+    loads[5].wait()
 
     def forward_slots(c, total):
         for lap in range(4):
@@ -259,6 +281,9 @@
         return total
 
     lax.fori_loop(0, 6, forward_slots, jnp.zeros((128, 256), F32))
+
+    loads[6].wait()
+    loads[7].wait()
 
     def node_update(c, sums):
         at = pl.ds(pl.multiple_of(c * 256, 256), 256)
@@ -288,7 +313,9 @@
         )
 
     zero_row = jnp.zeros((1, 256), F32)
-    bias_sum, gain_sum = lax.fori_loop(0, node_rows // 256, node_update, (zero_row, zero_row))
+    bias_sum, gain_sum = lax.fori_loop(
+        0, node_rows // 256, node_update, (zero_row, zero_row), unroll=2
+    )
 
     stores[0].start()
 
@@ -319,7 +346,7 @@
         for g in range(plane):
             stage_e[rep * plane + g, 48:64, :] = both
 
-    pl.semaphore_wait(pltpu.get_barrier_semaphore(), team + depth)
+    pl.semaphore_wait(pltpu.get_barrier_semaphore(), team + depth + plane - 1)
     to_team(stage_e, land_e, 0)
 
     def backward_slots(c, total):
@@ -332,11 +359,10 @@
 
     carried = lax.fori_loop(0, 4, backward_slots, jnp.zeros((128, 256), F32))
 
-    @pl.loop(0, peers)
-    def _(k):
-        back = (run[meta_s[7, k]] * halo_slope[k]).astype(BF16)
-        halo_grad[k] = back
-        rout[k] = dot_right_t(back, wm_ref[...]).astype(BF16)
+    for k in range(peers):
+        halo_grad[k] = (run[meta_s[7, k]] * halo_slope[k]).astype(BF16)
+    halo_back = halo_grad[...].reshape(peers * 128, 256)
+    rout[...] = dot_right_t(halo_back, wm_ref[...]).astype(BF16).reshape(peers, 128, 256)
 
     rin[2 + rep_at] = rout[2 + rep_at]
     send(rout.at[0], rin.at[0], 1, loop_down)
@@ -353,8 +379,7 @@
         own_grad[at, :] = (run[meta_s[7, peers + b]] * own_slope[at, :]).astype(BF16)
 
     message_grad = inner_rows(nf_ref[...], own_grad[...])
-    for k in range(peers):
-        message_grad += inner_rows(hin[k], halo_grad[k])
+    message_grad += inner_rows(hin[...].reshape(peers * 128, 256), halo_grad[...].reshape(peers * 128, 256))
     deal(stage_l, 0, 1, message_grad)
     to_team(stage_l, land_l, 2)
 
@@ -371,18 +396,13 @@
 
     arrived(land_e, 0)
     total = added(land_e, team)
-    vec_row = total[48:49]
+    vec_rows = jnp.broadcast_to(total[48:49], (8, 128))
     total = jnp.concatenate([total[64 * tile : 64 * tile + 48] for tile in range(sub)], axis=0)
-    rows = 48 * sub // depth
-    for z in range(depth):
-        zsend[z, 0:rows, :] = total[z * rows : (z + 1) * rows]
-        zsend[z, rows : rows + 1, :] = vec_row
-    zland[z_at] = zsend[z_at]
-
-    @pl.loop(1, depth)
-    def _(step):
-        z_to, device = above(step)
-        send(zsend.at[z_to], zland.at[z_at], 3, device)
+    rows = 24 * sub
+    for part in range(2):
+        psend[part, 0:rows, :] = total[part * rows : (part + 1) * rows]
+        psend[part, rows:, :] = vec_rows
+    send(psend.at[1 - parity], pland, 3, {"loop": z_pair * plane + g_at, "rep": rep_at})
 
     arrived(land_l, 2)
     lpiece[...] = added(land_l, team).astype(BF16)
@@ -390,75 +410,96 @@
 
     @pl.loop(1, depth)
     def _(step):
-        send(lpiece, lland.at[z_at], 4, above(step)[1])
+        send(lpiece, lland.at[z_at], 5, above(step)[1])
+
+    copy_all(pland, recv_sem.at[3]).wait()
+    total = psend[parity] + pland[...]
+    filler = jnp.zeros((epiece.shape[0] - total.shape[0], 128), F32)
+    epiece[...] = (jnp.concatenate([total, filler], axis=0) if filler.shape[0] else total).astype(BF16)
+    eland[z_at // 2] = epiece[...]
+
+    @pl.loop(1, depth // 2)
+    def _(step):
+        send(epiece, eland.at[z_at // 2], 4, above(2 * step)[1])
 
     arrived(rin, 1)
+    returned = rin[...].reshape(peers * 128, 256)
 
     @pl.loop(0, node_rows // 256)
     def _(c):
         at = pl.ds(pl.multiple_of(c * 256, 256), 256)
-        total = base[at, :]
-        for k in range(peers):
-            total += dot(spread[at, 128 * k : 128 * k + 128], rin[k])
-        out_grad[at, :] = total.astype(BF16)
+        out_grad[at, :] = (base[at, :] + dot(spread[at, :], returned)).astype(BF16)
 
     stores[1].start()
-    arrived(zland, 3)
-    total = added(zland, depth) * scale
+
+    arrived(lland, 5)
+    gpiece_l[...] = (added(lland, depth) * scale).astype(BF16)
+    to_plane(gpiece_l, gather_l, 6)
+
+    arrived(eland, 4)
+    total = added(eland, depth // 2) * scale
     vec_row = total[rows : rows + 1]
     half = out_bias.shape[1]
     out_bias[...] = vec_row[:, 0:half]
     out_gain[...] = pltpu.roll(vec_row, half, 1)[:, 0:half]
     stores[4].start()
     stores[6].start()
-    zpiece[...] = total
-    zgather[z_at] = total
-
-    @pl.loop(1, depth)
+    gpiece_e[...] = total.astype(BF16)
+    gather_e[parity * plane + g_at] = gpiece_e[...]
+
+    @pl.loop(1, 2 * plane)
     def _(step):
-        send(zpiece, zgather.at[z_at], 5, above(step)[1])
-
-    arrived(lland, 4)
-    gpiece_l[...] = (added(lland, depth) * scale).astype(BF16)
-    to_plane(gpiece_l, gather_l, 6)
-
-    arrived(zgather, 5)
-    gpiece_e[...] = jnp.concatenate([zgather[z, 0:rows, :] for z in range(depth)], axis=0).astype(BF16)
-    to_plane(gpiece_e, gather_e, 7)
-
-    def collect(out, gather, first, tall):
+        send(gpiece_e, gather_e.at[parity * plane + g_at], 7, twin(step))
+
+    def collect(out, owned, first, tall):
         for tile in range(8):
             row, half = 16 * tall * (tile // 2), 128 * (tile % 2)
-            slot, place = tile // sub, gather.shape[1] // sub * (tile % sub)
-            block = gather[slot, place + first : place + first + 16 * tall, :]
-            out[row : row + 16 * tall, half : half + 128] = block.astype(F32)
+            block = owned[tile // sub]
+            place = block.shape[0] // sub * (tile % sub) + first
+            out[row : row + 16 * tall, half : half + 128] = block[place : place + 16 * tall]
 
     arrived(gather_l, 6)
-    collect(out_mw, gather_l, 0, 1)
+    collect(out_mw, [gather_l[g].astype(F32) for g in range(plane)], 0, 1)
     stores[2].start()
     arrived(gather_e, 7)
-    collect(out_ow, gather_e, 0, 1)
+    owned = [
+        jnp.concatenate([gather_e[part * plane + g].astype(F32)[0:rows] for part in range(2)], axis=0)
+        for g in range(plane)
+    ]
+    collect(out_ow, owned, 0, 1)
     stores[5].start()
-    collect(out_iw, gather_e, 16, 2)
+    collect(out_iw, owned, 16, 2)
     stores[3].start()
 
-    sent = (land_e, rin, land_l, zland, lland, zgather, gather_l, gather_e)
-    for sem, land in enumerate(sent):
-        copy_all(land.at[1:], send_sem.at[sem]).wait()
+    for sem, land in ((0, land_e), (1, rin), (2, land_l), (4, eland), (5, lland), (6, gather_l), (7, gather_e)):
+        if land.shape[0] > 1:
+            copy_all(land.at[1:], send_sem.at[sem]).wait()
+    copy_all(pland, send_sem.at[3]).wait()
     for store in stores:
         store.wait()
 
 
 def finish_kernel(*refs):
-    sem = refs[-1]
-    copies = [
-        pltpu.make_async_copy(source, target, sem.at[i])
-        for i, (source, target) in enumerate(zip(refs[:7], refs[7:14]))
-    ]
-    for copy in copies:
-        copy.start()
-    for copy in copies:
-        copy.wait()
+    sources, targets, held, (load_sem, store_sem) = refs[:7], refs[7:14], refs[14:21], refs[21:]
+    pieces = []
+    for source, target, buffer in zip(sources, targets, held):
+        step = min(256, source.shape[0])
+        for first in range(0, source.shape[0], step):
+            at = pl.ds(first, step)
+            i = len(pieces)
+            pieces.append(
+                (
+                    pltpu.make_async_copy(source.at[at], buffer.at[at], load_sem.at[i]),
+                    pltpu.make_async_copy(buffer.at[at], target.at[at], store_sem.at[i]),
+                )
+            )
+    for load, _ in pieces:
+        load.start()
+    for load, store in pieces:
+        load.wait()
+        store.start()
+    for _, store in pieces:
+        store.wait()
 
 
 def shards(
@@ -482,8 +523,7 @@
     node_rows, width = node_features.shape
     blocks = node_rows // 128
     slots = adjacency.shape[2]
-    rows = 48 * sub // depth + 1
-    zrows = rows if rows <= 4 else -(-rows // 8) * 8
+    half_rows = -(-(24 * sub + 8) // 16) * 16
     scale = 1.0 / math.sqrt(node_rows * loop_size * reps)
     vmem, smem = pl.BlockSpec(memory_space=pltpu.VMEM), pl.BlockSpec(memory_space=pltpu.SMEM)
     hbm = pl.BlockSpec(memory_space=pltpu.HBM)
@@ -528,8 +568,8 @@
         scratch_shapes=[
             small,
             pltpu.VMEM((width, width), BF16),
+            pltpu.VMEM((2 * width, width), BF16),
             pltpu.VMEM((peers, 128, width), BF16),
-            pltpu.VMEM((2 * width, width), BF16),
             pltpu.SMEM((8, 128), jnp.int32),
             pltpu.VMEM((slots, 128, 128), BF16),
             small,
@@ -550,12 +590,12 @@
             pltpu.VMEM((peers, 128, width), BF16),
             pltpu.VMEM((reps * plane, 64 * sub, 128), BF16),
             pltpu.VMEM((reps * plane, 64 * sub, 128), BF16),
-            pltpu.VMEM((depth, zrows, 128), F32),
-            pltpu.VMEM((depth, zrows, 128), F32),
-            pltpu.VMEM((zrows, 128), F32),
-            pltpu.VMEM((depth, zrows, 128), F32),
-            pltpu.VMEM((48 * sub, 128), BF16),
-            pltpu.VMEM((plane, 48 * sub, 128), BF16),
+            pltpu.VMEM((2, 24 * sub + 8, 128), F32),
+            pltpu.VMEM((24 * sub + 8, 128), F32),
+            pltpu.VMEM((half_rows, 128), BF16),
+            pltpu.VMEM((depth // 2, half_rows, 128), BF16),
+            pltpu.VMEM((half_rows, 128), BF16),
+            pltpu.VMEM((2 * plane, half_rows, 128), BF16),
             pltpu.VMEM((reps * plane, 16 * sub, 128), BF16),
             pltpu.VMEM((reps * plane, 16 * sub, 128), BF16),
             pltpu.VMEM((16 * sub, 128), BF16),
@@ -574,8 +614,8 @@
     )(
         node_features,
         message_weight,
+        input_weight,
         hin,
-        input_weight,
         meta,
         adjacency[0, 0],
         cotangent,
@@ -590,7 +630,11 @@
         out_shape=results,
         in_specs=[hbm] * 7,
         out_specs=[hbm] * 7,
-        scratch_shapes=[pltpu.SemaphoreType.DMA((7,))],
+        scratch_shapes=[
+            *(pltpu.VMEM(result.shape, result.dtype) for result in results),
+            pltpu.SemaphoreType.DMA((16,)),
+            pltpu.SemaphoreType.DMA((16,)),
+        ],
         compiler_params=pltpu.CompilerParams(has_side_effects=True, vmem_limit_bytes=56 * mega),
         name="write_results",
     )(*outs)

time: 105 us -> 66.7 us (0.64)
  the two profiles are of different devices: /device:TPU:1 before, /device:TPU:2 now
where the time goes in v4:
time: 66.7 us; the launch traced here: 66.4 us
  Pallas kernels  65.1 us (98%)
  between operations  1.29 us (2%)
    pallas_call x1, Pallas kernels, shards(): pl.pallas_call(functools.partial(layer_kernel, plane, depth, reps, scale)...  42.6 us
    pallas_call x1, Pallas kernels, shards(): pl.pallas_call(functools.partial(halo_kernel, reps, loop_size), out_shape...  20.2 us
    pallas_call x1, Pallas kernels, shards(): pl.pallas_call(finish_kernel, out_shape=results, in_specs=[hbm] * 7, out_...  2.32 us

profile of v4, /device:TPU:2, one launch (start us, length us, event | category | flops | bytes accessed | tf_op | source)
XLA Modules:
  0.0 66.4 jit_solution(6532409734202338842)
XLA Ops:
  1.3 20.2 %halo_rows.1 = (bf16[6,128,256]{2,1,0:T(8,128)(2,1)}, s32[8,128]{1,0:T(8,128)}) custom-call(bf16[1024,256]{1,0:T(8,128)(2,1)} %nf_hbm.3, s32[2,24]{1,0:T(2,128)} %bitcast.13, s32[1,1]{1,0:T(1,128)S(6)} %copy.19.count_ref, s32[6,1,128]{2,1,0:T(1,128)} %bitcast.9, s32[1,6]{1,0:T(1,128)} %bitcast.11), custom_call_target="tpu_custom_call" | custom-call | tf_op jit(solution)/shard_map/halo_rows/pallas_call | solution.py:534
  21.5 42.6 %message_layer.1 = (bf16[1024,256]{1,0:T(8,128)(2,1)}, bf16[1024,256]{1,0:T(8,128)(2,1)}, f32[64,256]{1,0:T(8,128)}, f32[128,256]{1,0:T(8,128)}, f32[1,64]{1,0:T...) custom-call(bf16[1024,256]{1,0:T(8,128)(2,1)} %nf_hbm.3, bf16[256,256]{1,0:T(8,128)(2,1)} %wm_hbm.1, ...), custom_call_target="tpu_custom_call" | custom-call | tf_op jit(solution)/shard_map/message_layer/pallas_call | solution.py:563
  64.1 2.3 %write_results.1 = (bf16[1024,256]{1,0:T(8,128)(2,1)}, bf16[1024,256]{1,0:T(8,128)(2,1)}, f32[64,256]{1,0:T(8,128)}, f32[128,256]{1,0:T(8,128)}, f32[1,64]{1,0:T...) custom-call(bf16[1024,256]{1,0:T(8,128)(2,1)} %get-tuple-element.25.refs_0_, bf16[1024,256]{1,0:T(8,128)(2,1)} %get-tuple-element.26.refs_1_, ...), custom_call_target="tpu_custom_call" | custom-call | tf_op jit(solution)/shard_map/write_results/pallas_call | solution.py:628

commit v5 on v4

--- a/solution.py
+++ b/solution.py
@@ -61,7 +61,8 @@
 
 def silu_and_slope(pre):
     gate = sigmoid(pre)
-    return (pre * gate).astype(BF16), gate * (1.0 + pre * (1.0 - gate))
+    value = pre * gate
+    return value.astype(BF16), gate + value * (1.0 - gate)
 
 
 def remote(source, target, send_sem, recv_sem, device):
@@ -153,7 +154,7 @@
     nf_ref, wm_ref, wi_ref, hin, meta_s, adj_ref, cot_ref, wo_ref,
     out_new, out_grad, out_mw, out_iw, out_bias, out_ow, out_gain,
     rout, rin, table, own_slope, halo_slope, pre_part, spread, run,
-    agg, hidden, outer_grad, pre_grad, agg_grad, base, own_grad, halo_grad,
+    agg, hidden, outer_grad, pre_grad, agg_grad, norm_rows, own_grad, halo_grad,
     stage_e, land_e, psend, pland, epiece, eland, gpiece_e, gather_e,
     stage_l, land_l, lpiece, lland, gpiece_l, gather_l,
     load_sem, store_sem, send_sem, recv_sem,
@@ -253,7 +254,7 @@
     for load in loads[:3]:
         load.wait()
 
-    @pl.loop(0, node_rows // 256)
+    @pl.loop(0, node_rows // 256, unroll=2)
     def _(c):
         at = pl.ds(pl.multiple_of(c * 256, 256), 256)
         features = nf_ref[at, :]
@@ -280,12 +281,12 @@
             run[i] = total
         return total
 
-    lax.fori_loop(0, 6, forward_slots, jnp.zeros((128, 256), F32))
+    lax.fori_loop(0, 6, forward_slots, jnp.zeros((128, 256), F32), unroll=6)
 
     loads[6].wait()
     loads[7].wait()
 
-    def node_update(c, sums):
+    def node_update(c, gain_sum):
         at = pl.ds(pl.multiple_of(c * 256, 256), 256)
         gathered = jnp.concatenate(
             [run[meta_s[3, 2 * c]], run[meta_s[3, 2 * c + 1]]], axis=0
@@ -297,27 +298,17 @@
         centered = outer - row_mean(outer)
         inv_std = lax.rsqrt(row_mean(centered * centered) + norm_eps)
         normed = centered * inv_std
-        gain = gain_ref[...]
-        out_new[at, :] = (nf_ref[at, :].astype(F32) + normed * gain).astype(BF16)
+        norm_rows[at, :] = normed
         upstream = cot_ref[at, :].astype(F32)
-        gained = upstream * gain
+        gained = upstream * gain_ref[...]
         back = ((gained - row_mean(gained) - normed * row_mean(gained * normed)) * inv_std).astype(BF16)
         outer_grad[at, :] = back
-        back = (dot_right_t(back, wo_ref[...]) * hid_slope).astype(BF16)
-        pre_grad[at, :] = back
-        base[at, :] = upstream + dot_right_t(back, wi_ref[0:256, :])
-        agg_grad[pl.ds(2 * c, 2)] = dot_right_t(back, wi_ref[256:512, :]).astype(BF16).reshape(2, 128, 256)
-        return (
-            sums[0] + jnp.sum(back.astype(F32), axis=0, keepdims=True),
-            sums[1] + jnp.sum(upstream * normed, axis=0, keepdims=True),
-        )
-
-    zero_row = jnp.zeros((1, 256), F32)
-    bias_sum, gain_sum = lax.fori_loop(
-        0, node_rows // 256, node_update, (zero_row, zero_row), unroll=2
-    )
-
-    stores[0].start()
+        pre_grad[at, :] = (dot_right_t(back, wo_ref[...]) * hid_slope).astype(BF16)
+        return gain_sum + jnp.sum(upstream * normed, axis=0, keepdims=True)
+
+    gain_sum = lax.fori_loop(
+        0, node_rows // 256, node_update, jnp.zeros((1, 256), F32), unroll=2
+    )
 
     def deal(stage, first, tall, value):
         for rep in range(reps):
@@ -330,6 +321,7 @@
 
     deal(stage_e, 0, 1, inner_rows(hidden[...], outer_grad[...]))
     back_all = pre_grad[...]
+    bias_sum = dot(jnp.ones((16, node_rows), BF16), back_all)[0:1]
     deal(
         stage_e, 16, 2,
         jnp.concatenate([inner_rows(nf_ref[...], back_all), inner_rows(agg[...], back_all)], axis=0),
@@ -349,6 +341,12 @@
     pl.semaphore_wait(pltpu.get_barrier_semaphore(), team + depth + plane - 1)
     to_team(stage_e, land_e, 0)
 
+    @pl.loop(0, node_rows // 256, unroll=2)
+    def _(c):
+        at = pl.ds(pl.multiple_of(c * 256, 256), 256)
+        back = dot_right_t(pre_grad[at, :], wi_ref[256:512, :])
+        agg_grad[pl.ds(2 * c, 2)] = back.astype(BF16).reshape(2, 128, 256)
+
     def backward_slots(c, total):
         for lap in range(4):
             i = c * 4 + lap
@@ -357,10 +355,20 @@
             run[i] = total
         return total
 
-    carried = lax.fori_loop(0, 4, backward_slots, jnp.zeros((128, 256), F32))
+    lax.fori_loop(0, 6, backward_slots, jnp.zeros((128, 256), F32), unroll=6)
 
     for k in range(peers):
         halo_grad[k] = (run[meta_s[7, k]] * halo_slope[k]).astype(BF16)
+    @pl.loop(0, blocks, unroll=4)
+    def _(b):
+        at = pl.ds(pl.multiple_of(b * 128, 128), 128)
+        own_grad[at, :] = (run[meta_s[7, peers + b]] * own_slope[at, :]).astype(BF16)
+
+    message_grad = inner_rows(nf_ref[...], own_grad[...])
+    message_grad += inner_rows(hin[...].reshape(peers * 128, 256), halo_grad[...].reshape(peers * 128, 256))
+    deal(stage_l, 0, 1, message_grad)
+    to_team(stage_l, land_l, 2)
+
     halo_back = halo_grad[...].reshape(peers * 128, 256)
     rout[...] = dot_right_t(halo_back, wm_ref[...]).astype(BF16).reshape(peers, 128, 256)
 
@@ -370,23 +378,6 @@
     for step in range(1, reps):
         r_to = lax.rem(rep_at + step, reps)
         send(rout.at[2 + r_to], rin.at[2 + rep_at], 1, {"loop": loop_at, "rep": r_to})
-
-    lax.fori_loop(4, 6, backward_slots, carried)
-
-    @pl.loop(0, blocks)
-    def _(b):
-        at = pl.ds(pl.multiple_of(b * 128, 128), 128)
-        own_grad[at, :] = (run[meta_s[7, peers + b]] * own_slope[at, :]).astype(BF16)
-
-    message_grad = inner_rows(nf_ref[...], own_grad[...])
-    message_grad += inner_rows(hin[...].reshape(peers * 128, 256), halo_grad[...].reshape(peers * 128, 256))
-    deal(stage_l, 0, 1, message_grad)
-    to_team(stage_l, land_l, 2)
-
-    @pl.loop(0, node_rows // 256)
-    def _(c):
-        at = pl.ds(pl.multiple_of(c * 256, 256), 256)
-        base[at, :] += dot_right_t(own_grad[at, :], wm_ref[...])
 
     row_at = lax.broadcasted_iota(jnp.int32, (node_rows, 128), 0)
     lane_at = lax.broadcasted_iota(jnp.int32, (node_rows, 128), 1)
@@ -425,11 +416,15 @@
     arrived(rin, 1)
     returned = rin[...].reshape(peers * 128, 256)
 
-    @pl.loop(0, node_rows // 256)
+    @pl.loop(0, node_rows // 256, unroll=2)
     def _(c):
         at = pl.ds(pl.multiple_of(c * 256, 256), 256)
-        out_grad[at, :] = (base[at, :] + dot(spread[at, :], returned)).astype(BF16)
-
+        out_new[at, :] = (nf_ref[at, :].astype(F32) + norm_rows[at, :] * gain_ref[...]).astype(BF16)
+        total = cot_ref[at, :].astype(F32) + dot_right_t(pre_grad[at, :], wi_ref[0:256, :])
+        total += dot_right_t(own_grad[at, :], wm_ref[...])
+        out_grad[at, :] = (total + dot(spread[at, :], returned)).astype(BF16)
+
+    stores[0].start()
     stores[1].start()
 
     arrived(lland, 5)

time: 66.7 us -> 62 us (0.930)
  the two profiles are of different devices: /device:TPU:2 before, /device:TPU:1 now
where the time goes in v5:
time: 62 us; the launch traced here: 61.7 us
  Pallas kernels  60.4 us (97%)
  between operations  1.29 us (2%)
    pallas_call x1, Pallas kernels, shards(): pl.pallas_call(functools.partial(layer_kernel, plane, depth, reps, scale)...  36.3 us
    pallas_call x1, Pallas kernels, shards(): pl.pallas_call(functools.partial(halo_kernel, reps, loop_size), out_shape...  21.8 us
    pallas_call x1, Pallas kernels, shards(): pl.pallas_call(finish_kernel, out_shape=results, in_specs=[hbm] * 7, out_...  2.32 us

profile of v5, /device:TPU:1, one launch (start us, length us, event | category | flops | bytes accessed | tf_op | source)
XLA Modules:
  0.0 61.7 jit_solution(7063557754110071763)
XLA Ops:
  1.3 21.8 %halo_rows.1 = (bf16[6,128,256]{2,1,0:T(8,128)(2,1)}, s32[8,128]{1,0:T(8,128)}) custom-call(bf16[1024,256]{1,0:T(8,128)(2,1)} %nf_hbm.3, s32[2,24]{1,0:T(2,128)} %bitcast.13, s32[1,1]{1,0:T(1,128)S(6)} %copy.19.count_ref, s32[6,1,128]{2,1,0:T(1,128)} %bitcast.9, s32[1,6]{1,0:T(1,128)} %bitcast.11), custom_call_target="tpu_custom_call" | custom-call | tf_op jit(solution)/shard_map/halo_rows/pallas_call | solution.py:529
  23.0 36.3 %message_layer.1 = (bf16[1024,256]{1,0:T(8,128)(2,1)}, bf16[1024,256]{1,0:T(8,128)(2,1)}, f32[64,256]{1,0:T(8,128)}, f32[128,256]{1,0:T(8,128)}, f32[1,64]{1,0:T...) custom-call(bf16[1024,256]{1,0:T(8,128)(2,1)} %nf_hbm.3, bf16[256,256]{1,0:T(8,128)(2,1)} %wm_hbm.1, ...), custom_call_target="tpu_custom_call" | custom-call | tf_op jit(solution)/shard_map/message_layer/pallas_call | solution.py:558
  59.4 2.3 %write_results.1 = (bf16[1024,256]{1,0:T(8,128)(2,1)}, bf16[1024,256]{1,0:T(8,128)(2,1)}, f32[64,256]{1,0:T(8,128)}, f32[128,256]{1,0:T(8,128)}, f32[1,64]{1,0:T...) custom-call(bf16[1024,256]{1,0:T(8,128)(2,1)} %get-tuple-element.25.refs_0_, bf16[1024,256]{1,0:T(8,128)(2,1)} %get-tuple-element.26.refs_1_, ...), custom_call_target="tpu_custom_call" | custom-call | tf_op jit(solution)/shard_map/write_results/pallas_call | solution.py:623

commit v6 on v5

--- a/solution.py
+++ b/solution.py
@@ -77,9 +77,9 @@
 
 def halo_kernel(
     reps, loop_size,
-    nf_hbm, index_ref, count_ref, rows_ref, kept_ref,
-    hin, meta,
-    nf_ref, flat, hout, load_sem, send_sem, recv_sem,
+    nf_hbm, wm_hbm, index_ref, count_ref, rows_ref, kept_ref,
+    hin, messages, meta,
+    nf_ref, wm_ref, flat, hout, held, load_sem, send_sem, recv_sem,
 ):
     node_rows = nf_ref.shape[0]
     blocks = node_rows // 128
@@ -88,8 +88,10 @@
     loop_up = {"loop": lax.rem(loop_at + 1, loop_size), "rep": rep_at}
     loop_down = {"loop": lax.rem(loop_at + loop_size - 1, loop_size), "rep": rep_at}
 
-    load = pltpu.make_async_copy(nf_hbm, nf_ref, load_sem)
+    load = pltpu.make_async_copy(nf_hbm, nf_ref, load_sem.at[0])
     load.start()
+    load_wm = pltpu.make_async_copy(wm_hbm, wm_ref, load_sem.at[1])
+    load_wm.start()
     greet(loop_up)
     greet(loop_down)
     for step in range(1, reps):
@@ -120,8 +122,14 @@
         remote(
             hout.at[2 + r_to], hin.at[2 + rep_at], send_sem, recv_sem, {"loop": loop_at, "rep": r_to}
         )
-    own = pltpu.make_async_copy(hout.at[2 + rep_at], hin.at[2 + rep_at], load_sem)
+    own = pltpu.make_async_copy(hout.at[2 + rep_at], hin.at[2 + rep_at], load_sem.at[2])
     own.start()
+
+    load_wm.wait()
+    value, _ = silu_and_slope(dot(nf_ref[...], wm_ref[...]))
+    held[...] = value.reshape(blocks, 128, 256)
+    store = pltpu.make_async_copy(held, messages, load_sem.at[3])
+    store.start()
 
     live_total = count_ref[0, 0]
     slot_col = lax.broadcasted_iota(jnp.int32, (32, 1), 0)
@@ -142,18 +150,19 @@
     meta[...] = jnp.concatenate(forward + backward, axis=0)
 
     own.wait()
+    store.wait()
     copy_all(hin.at[1:], recv_sem).wait()
     copy_all(hin.at[1:], send_sem).wait()
 
 
 def layer_kernel(
     plane, depth, reps, scale,
-    nf_hbm, wm_hbm, wi_hbm, hin_hbm, meta_hbm, adj_hbm, cot_hbm, wo_hbm,
+    messages_hbm, hin_hbm, wm_hbm, meta_hbm, adj_hbm, nf_hbm, wi_hbm, wo_hbm, cot_hbm,
     rows_ref, kept_ref, bias_ref, gain_ref,
     new_hbm, grad_hbm, mw_hbm, iw_hbm, grad_bias_hbm, ow_hbm, grad_gain_hbm,
-    nf_ref, wm_ref, wi_ref, hin, meta_s, adj_ref, cot_ref, wo_ref,
+    table, hin, wm_ref, meta_s, adj_ref, nf_ref, wi_ref, wo_ref, cot_ref,
     out_new, out_grad, out_mw, out_iw, out_bias, out_ow, out_gain,
-    rout, rin, table, own_slope, halo_slope, pre_part, spread, run,
+    rout, rin, halo_slope, spread, run,
     agg, hidden, outer_grad, pre_grad, agg_grad, norm_rows, own_grad, halo_grad,
     stage_e, land_e, psend, pland, epiece, eland, gpiece_e, gather_e,
     stage_l, land_l, lpiece, lland, gpiece_l, gather_l,
@@ -219,8 +228,9 @@
         pltpu.make_async_copy(source, target, load_sem.at[i])
         for i, (source, target) in enumerate(
             (
-                (nf_hbm, nf_ref), (wm_hbm, wm_ref), (wi_hbm, wi_ref), (hin_hbm, hin),
-                (meta_hbm, meta_s), (adj_hbm, adj_ref), (cot_hbm, cot_ref), (wo_hbm, wo_ref),
+                (messages_hbm, table.at[0:blocks]), (hin_hbm, hin), (wm_hbm, wm_ref),
+                (meta_hbm, meta_s), (adj_hbm, adj_ref), (nf_hbm, nf_ref), (wi_hbm, wi_ref),
+                (wo_hbm, wo_ref), (cot_hbm, cot_ref),
             )
         )
     ]
@@ -251,18 +261,8 @@
     greet(loop_up)
     greet(loop_down)
 
-    for load in loads[:3]:
-        load.wait()
-
-    @pl.loop(0, node_rows // 256, unroll=2)
-    def _(c):
-        at = pl.ds(pl.multiple_of(c * 256, 256), 256)
-        features = nf_ref[at, :]
-        message, own_slope[at, :] = silu_and_slope(dot(features, wm_ref[...]))
-        table[pl.ds(2 * c, 2)] = message.reshape(2, 128, 256)
-        pre_part[at, :] = dot(features, wi_ref[0:256, :]) + bias_ref[...]
-
-    loads[3].wait()
+    loads[1].wait()
+    loads[2].wait()
     half_peers = peers // 2
     for first in range(0, peers, half_peers):
         some = slice(first, first + half_peers)
@@ -270,8 +270,8 @@
         table[blocks + first : blocks + first + half_peers] = message.reshape(half_peers, 128, 256)
         halo_slope[some] = gate.reshape(half_peers, 128, 256)
 
-    loads[4].wait()
-    loads[5].wait()
+    for load in (loads[0], loads[3], loads[4]):
+        load.wait()
 
     def forward_slots(c, total):
         for lap in range(4):
@@ -283,8 +283,8 @@
 
     lax.fori_loop(0, 6, forward_slots, jnp.zeros((128, 256), F32), unroll=6)
 
-    loads[6].wait()
-    loads[7].wait()
+    for load in loads[5:]:
+        load.wait()
 
     def node_update(c, gain_sum):
         at = pl.ds(pl.multiple_of(c * 256, 256), 256)
@@ -292,7 +292,8 @@
             [run[meta_s[3, 2 * c]], run[meta_s[3, 2 * c + 1]]], axis=0
         ).astype(BF16)
         agg[at, :] = gathered
-        hid, hid_slope = silu_and_slope(pre_part[at, :] + dot(gathered, wi_ref[256:512, :]))
+        pre = dot(nf_ref[at, :], wi_ref[0:256, :]) + bias_ref[...]
+        hid, hid_slope = silu_and_slope(pre + dot(gathered, wi_ref[256:512, :]))
         hidden[at, :] = hid
         outer = dot(hid, wo_ref[...])
         centered = outer - row_mean(outer)
@@ -362,22 +363,13 @@
     @pl.loop(0, blocks, unroll=4)
     def _(b):
         at = pl.ds(pl.multiple_of(b * 128, 128), 128)
-        own_grad[at, :] = (run[meta_s[7, peers + b]] * own_slope[at, :]).astype(BF16)
+        _, own_slope = silu_and_slope(dot(nf_ref[at, :], wm_ref[...]))
+        own_grad[at, :] = (run[meta_s[7, peers + b]] * own_slope).astype(BF16)
 
     message_grad = inner_rows(nf_ref[...], own_grad[...])
     message_grad += inner_rows(hin[...].reshape(peers * 128, 256), halo_grad[...].reshape(peers * 128, 256))
     deal(stage_l, 0, 1, message_grad)
     to_team(stage_l, land_l, 2)
-
-    halo_back = halo_grad[...].reshape(peers * 128, 256)
-    rout[...] = dot_right_t(halo_back, wm_ref[...]).astype(BF16).reshape(peers, 128, 256)
-
-    rin[2 + rep_at] = rout[2 + rep_at]
-    send(rout.at[0], rin.at[0], 1, loop_down)
-    send(rout.at[1], rin.at[1], 1, loop_up)
-    for step in range(1, reps):
-        r_to = lax.rem(rep_at + step, reps)
-        send(rout.at[2 + r_to], rin.at[2 + rep_at], 1, {"loop": loop_at, "rep": r_to})
 
     row_at = lax.broadcasted_iota(jnp.int32, (node_rows, 128), 0)
     lane_at = lax.broadcasted_iota(jnp.int32, (node_rows, 128), 1)
@@ -402,6 +394,16 @@
     @pl.loop(1, depth)
     def _(step):
         send(lpiece, lland.at[z_at], 5, above(step)[1])
+
+    halo_back = halo_grad[...].reshape(peers * 128, 256)
+    rout[...] = dot_right_t(halo_back, wm_ref[...]).astype(BF16).reshape(peers, 128, 256)
+
+    rin[2 + rep_at] = rout[2 + rep_at]
+    send(rout.at[0], rin.at[0], 1, loop_down)
+    send(rout.at[1], rin.at[1], 1, loop_up)
+    for step in range(1, reps):
+        r_to = lax.rem(rep_at + step, reps)
+        send(rout.at[2 + r_to], rin.at[2 + rep_at], 1, {"loop": loop_at, "rep": r_to})
 
     copy_all(pland, recv_sem.at[3]).wait()
     total = psend[parity] + pland[...]
@@ -526,16 +528,22 @@
     wide = (node_rows, width)
     mega = 1024 * 1024
     rows_in = send_rows.reshape(peers, 1, 128)
-    hin, meta = pl.pallas_call(
+    hin, messages, meta = pl.pallas_call(
         functools.partial(halo_kernel, reps, loop_size),
-        out_shape=(shape((peers, 128, width), BF16), shape((8, 128), jnp.int32)),
-        in_specs=[hbm, vmem, smem, vmem, smem],
-        out_specs=[hbm, vmem],
+        out_shape=(
+            shape((peers, 128, width), BF16),
+            shape((blocks, 128, width), BF16),
+            shape((8, 128), jnp.int32),
+        ),
+        in_specs=[hbm, hbm, vmem, smem, vmem, smem],
+        out_specs=[hbm, hbm, vmem],
         scratch_shapes=[
             pltpu.VMEM(wide, BF16),
+            pltpu.VMEM((width, width), BF16),
             pltpu.VMEM((128, 128), jnp.int32),
             pltpu.VMEM((peers, 128, width), BF16),
-            pltpu.SemaphoreType.DMA,
+            pltpu.VMEM((blocks, 128, width), BF16),
+            pltpu.SemaphoreType.DMA((4,)),
             pltpu.SemaphoreType.DMA,
             pltpu.SemaphoreType.DMA,
         ],
@@ -543,7 +551,7 @@
             collective_id=0, has_side_effects=True, vmem_limit_bytes=56 * mega
         ),
         name="halo_rows",
-    )(node_features, block_index[0, 0], block_count, rows_in, row_counts[0])
+    )(node_features, message_weight, block_index[0, 0], block_count, rows_in, row_counts[0])
     small = pltpu.VMEM(wide, BF16)
     half = width // reps
     results = (
@@ -558,24 +566,22 @@
     outs = pl.pallas_call(
         functools.partial(layer_kernel, plane, depth, reps, scale),
         out_shape=results,
-        in_specs=[hbm] * 8 + [vmem, smem, vmem, vmem],
+        in_specs=[hbm] * 9 + [vmem, smem, vmem, vmem],
         out_specs=[hbm] * 7,
         scratch_shapes=[
-            small,
+            pltpu.VMEM((blocks + peers, 128, width), BF16),
+            pltpu.VMEM((peers, 128, width), BF16),
             pltpu.VMEM((width, width), BF16),
-            pltpu.VMEM((2 * width, width), BF16),
-            pltpu.VMEM((peers, 128, width), BF16),
             pltpu.SMEM((8, 128), jnp.int32),
             pltpu.VMEM((slots, 128, 128), BF16),
             small,
+            pltpu.VMEM((2 * width, width), BF16),
             pltpu.VMEM((width, width), BF16),
+            small,
             *(pltpu.VMEM(result.shape, result.dtype) for result in results),
             pltpu.VMEM((peers, 128, width), BF16),
             pltpu.VMEM((peers, 128, width), BF16),
-            pltpu.VMEM((blocks + peers, 128, width), BF16),
-            pltpu.VMEM(wide, F32),
             pltpu.VMEM((peers, 128, width), F32),
-            pltpu.VMEM(wide, F32),
             pltpu.VMEM((node_rows, peers * 128), BF16),
             pltpu.VMEM((slots, 128, width), F32),
             small, small, small, small,
@@ -597,7 +603,7 @@
             pltpu.VMEM((depth, 16 * sub, 128), BF16),
             pltpu.VMEM((16 * sub, 128), BF16),
             pltpu.VMEM((plane, 16 * sub, 128), BF16),
-            pltpu.SemaphoreType.DMA((8,)),
+            pltpu.SemaphoreType.DMA((9,)),
             pltpu.SemaphoreType.DMA((7,)),
             pltpu.SemaphoreType.DMA((8,)),
             pltpu.SemaphoreType.DMA((8,)),
@@ -607,14 +613,15 @@
         ),
         name="message_layer",
     )(
-        node_features,
+        messages,
+        hin,
         message_weight,
-        input_weight,
-        hin,
         meta,
         adjacency[0, 0],
+        node_features,
+        input_weight,
+        output_weight,
         cotangent,
-        output_weight,
         rows_in,
         row_counts[0],
         input_bias[None, :],

time: 62 us -> 61.2 us (0.987); the launches traced: 61.7 us -> 60.2 us
  Pallas kernels: 60.4 us -> 58.9 us
    pallas_call x1, Pallas kernels: 36.3 us -> 34.8 us  [shards(): pl.pallas_call(functools.partial(layer_kernel, plane, depth, reps, scale)...]
where the time goes in v6:
time: 61.2 us; the launch traced here: 60.2 us
  Pallas kernels  58.9 us (96%)
  between operations  1.29 us (2%)
    pallas_call x1, Pallas kernels, shards(): pl.pallas_call(functools.partial(layer_kernel, plane, depth, reps, scale)...  34.8 us
    pallas_call x1, Pallas kernels, shards(): pl.pallas_call(functools.partial(halo_kernel, reps, loop_size), out_shape...  21.8 us
    pallas_call x1, Pallas kernels, shards(): pl.pallas_call(finish_kernel, out_shape=results, in_specs=[hbm] * 7, out_...  2.32 us

profile of v6, /device:TPU:1, one launch (start us, length us, event | category | flops | bytes accessed | tf_op | source)
XLA Modules:
  0.0 60.2 jit_solution(5604569161127763743)
XLA Ops:
  1.3 21.8 %halo_rows.1 = (bf16[6,128,256]{2,1,0:T(8,128)(2,1)}, bf16[8,128,256]{2,1,0:T(8,128)(2,1)}, s32[8,128]{1,0:T(8,128)}) custom-call(bf16[1024,256]{1,0:T(8,128)(2,1)} %nf_hbm.3, bf16[256,256]{1,0:T(8,128)(2,1)} %wm_hbm.3, s32[2,24]{1,0:T(2,128)} %bitcast.15, s32[1,1]{1,0:T(1,128)S(6)} %copy.19.count_ref, s32[6,1,128]{2,1,0:T(1,128)} %bitcast.9, s32[1,6]{1,0:T(1,128)} %bitcast.11), custom_call_target="tpu_custom_call" | custom-call | tf_op jit(solution)/shard_map/halo_rows/pallas_call | solution.py:531
  23.1 34.8 %message_layer.1 = (bf16[1024,256]{1,0:T(8,128)(2,1)}, bf16[1024,256]{1,0:T(8,128)(2,1)}, f32[64,256]{1,0:T(8,128)}, f32[128,256]{1,0:T(8,128)}, f32[1,64]{1,0:T...) custom-call(bf16[8,128,256]{2,1,0:T(8,128)(2,1)} %get-tuple-element.24.messages_hbm, ...), custom_call_target="tpu_custom_call" | custom-call | tf_op jit(solution)/shard_map/message_layer/pallas_call | solution.py:566
  57.9 2.3 %write_results.1 = (bf16[1024,256]{1,0:T(8,128)(2,1)}, bf16[1024,256]{1,0:T(8,128)(2,1)}, f32[64,256]{1,0:T(8,128)}, f32[128,256]{1,0:T(8,128)}, f32[1,64]{1,0:T...) custom-call(bf16[1024,256]{1,0:T(8,128)(2,1)} %get-tuple-element.27.refs_0_, bf16[1024,256]{1,0:T(8,128)(2,1)} %get-tuple-element.28.refs_1_, ...), custom_call_target="tpu_custom_call" | custom-call | tf_op jit(solution)/shard_map/write_results/pallas_call | solution.py:630

commit v7 on v6

--- a/solution.py
+++ b/solution.py
@@ -75,98 +75,19 @@
     pl.semaphore_signal(pltpu.get_barrier_semaphore(), inc=1, device_id=device, device_id_type=MESH)
 
 
-def halo_kernel(
-    reps, loop_size,
-    nf_hbm, wm_hbm, index_ref, count_ref, rows_ref, kept_ref,
-    hin, messages, meta,
-    nf_ref, wm_ref, flat, hout, held, load_sem, send_sem, recv_sem,
-):
-    node_rows = nf_ref.shape[0]
-    blocks = node_rows // 128
-    peers = 2 + reps
-    loop_at, rep_at = lax.axis_index("loop"), lax.axis_index("rep")
-    loop_up = {"loop": lax.rem(loop_at + 1, loop_size), "rep": rep_at}
-    loop_down = {"loop": lax.rem(loop_at + loop_size - 1, loop_size), "rep": rep_at}
-
-    load = pltpu.make_async_copy(nf_hbm, nf_ref, load_sem.at[0])
-    load.start()
-    load_wm = pltpu.make_async_copy(wm_hbm, wm_ref, load_sem.at[1])
-    load_wm.start()
-    greet(loop_up)
-    greet(loop_down)
-    for step in range(1, reps):
-        greet({"loop": loop_at, "rep": lax.rem(rep_at + step, reps)})
-    flat[...] = jnp.zeros(flat.shape, jnp.int32)
-    flat[0:2, 0:24] = index_ref[...]
-    for k in range(peers):
-        flat[8 + k : 9 + k, :] = rows_ref[k]
-    turned = jnp.transpose(flat[...])
-    lane_rows = lax.broadcasted_iota(jnp.int32, (128, node_rows), 1)
-    sub_rows = lax.broadcasted_iota(jnp.int32, (128, node_rows), 0)
-    load.wait()
-
-    def pick(k):
-        live = (lane_rows == turned[:, 8 + k : 9 + k]) & (sub_rows < kept_ref[0, k])
-        picker = jnp.where(live, 1.0, 0.0).astype(BF16)
-        hout[k] = dot(picker, nf_ref[...]).astype(BF16)
-
-    pick(0)
-    pick(1)
-    pl.semaphore_wait(pltpu.get_barrier_semaphore(), 1 + reps)
-    remote(hout.at[0], hin.at[0], send_sem, recv_sem, loop_up)
-    remote(hout.at[1], hin.at[1], send_sem, recv_sem, loop_down)
-    for k in range(2, peers):
-        pick(k)
-    for step in range(1, reps):
-        r_to = lax.rem(rep_at + step, reps)
-        remote(
-            hout.at[2 + r_to], hin.at[2 + rep_at], send_sem, recv_sem, {"loop": loop_at, "rep": r_to}
-        )
-    own = pltpu.make_async_copy(hout.at[2 + rep_at], hin.at[2 + rep_at], load_sem.at[2])
-    own.start()
-
-    load_wm.wait()
-    value, _ = silu_and_slope(dot(nf_ref[...], wm_ref[...]))
-    held[...] = value.reshape(blocks, 128, 256)
-    store = pltpu.make_async_copy(held, messages, load_sem.at[3])
-    store.start()
-
-    live_total = count_ref[0, 0]
-    slot_col = lax.broadcasted_iota(jnp.int32, (32, 1), 0)
-    slot_row = lax.broadcasted_iota(jnp.int32, (1, 128), 1)
-    dest_col, source_col = turned[0:32, 0:1], turned[0:32, 1:2]
-    dest_row, source_row = flat[0:1, :], flat[1:2, :]
-
-    def keyed(value, iota):
-        return jnp.where(iota < live_total, value, 64)
-
-    def halo_first(value):
-        return jnp.where(value >= blocks, value - blocks, value + peers)
-
-    forward = slot_order(keyed(dest_col, slot_col), keyed(dest_row, slot_row), (source_col,))
-    backward = slot_order(
-        keyed(halo_first(source_col), slot_col), keyed(halo_first(source_row), slot_row), (dest_col,)
-    )
-    meta[...] = jnp.concatenate(forward + backward, axis=0)
-
-    own.wait()
-    store.wait()
-    copy_all(hin.at[1:], recv_sem).wait()
-    copy_all(hin.at[1:], send_sem).wait()
-
-
 def layer_kernel(
     plane, depth, reps, scale,
-    messages_hbm, hin_hbm, wm_hbm, meta_hbm, adj_hbm, nf_hbm, wi_hbm, wo_hbm, cot_hbm,
-    rows_ref, kept_ref, bias_ref, gain_ref,
+    nf_hbm, wm_hbm, adj_hbm, wi_hbm, wo_hbm, cot_hbm,
+    index_ref, count_ref, rows_ref, kept_ref, bias_ref, gain_ref,
     new_hbm, grad_hbm, mw_hbm, iw_hbm, grad_bias_hbm, ow_hbm, grad_gain_hbm,
-    table, hin, wm_ref, meta_s, adj_ref, nf_ref, wi_ref, wo_ref, cot_ref,
+    nf_ref, wm_ref, adj_ref, wi_ref, wo_ref, cot_ref,
+    flat, meta_v, meta_s, hout, hin, table,
     out_new, out_grad, out_mw, out_iw, out_bias, out_ow, out_gain,
     rout, rin, halo_slope, spread, run,
     agg, hidden, outer_grad, pre_grad, agg_grad, norm_rows, own_grad, halo_grad,
     stage_e, land_e, psend, pland, epiece, eland, gpiece_e, gather_e,
     stage_l, land_l, lpiece, lland, gpiece_l, gather_l,
-    load_sem, store_sem, send_sem, recv_sem,
+    load_sem, store_sem, meta_sem, relay_sem, send_sem, recv_sem,
 ):
     sub = 8 // plane
     node_rows = nf_ref.shape[0]
@@ -189,6 +110,9 @@
         z_to = lax.rem(z_at + step, depth)
         return z_to, {"loop": z_to * plane + g_at, "rep": rep_at}
 
+    near = max(1, depth // 4)
+    near_steps = sorted({side for k in range(1, near + 1) for side in (k, depth - k)})
+    relay_steps = sorted({near, depth - near})
     parity = lax.rem(z_at, 2)
     z_pair = z_at + 1 - 2 * parity
 
@@ -228,9 +152,8 @@
         pltpu.make_async_copy(source, target, load_sem.at[i])
         for i, (source, target) in enumerate(
             (
-                (messages_hbm, table.at[0:blocks]), (hin_hbm, hin), (wm_hbm, wm_ref),
-                (meta_hbm, meta_s), (adj_hbm, adj_ref), (nf_hbm, nf_ref), (wi_hbm, wi_ref),
-                (wo_hbm, wo_ref), (cot_hbm, cot_ref),
+                (nf_hbm, nf_ref), (wm_hbm, wm_ref), (adj_hbm, adj_ref),
+                (wi_hbm, wi_ref), (wo_hbm, wo_ref), (cot_hbm, cot_ref),
             )
         )
     ]
@@ -246,23 +169,74 @@
         )
     ]
 
-    @pl.loop(1, depth)
-    def _(step):
+    greet(loop_up)
+    greet(loop_down)
+    for step in near_steps:
         greet(above(step)[1])
 
     @pl.loop(1, team)
     def _(step):
         greet(mate(step)[1])
 
-    @pl.loop(1, plane)
-    def _(step):
-        greet({"loop": z_pair * plane + lax.rem(g_at + step, plane), "rep": rep_at})
-
-    greet(loop_up)
-    greet(loop_down)
+    flat[...] = jnp.zeros(flat.shape, jnp.int32)
+    flat[0:2, 0:24] = index_ref[...]
+    for k in range(peers):
+        flat[8 + k : 9 + k, :] = rows_ref[k]
+    turned = jnp.transpose(flat[...])
+    lane_rows = lax.broadcasted_iota(jnp.int32, (128, node_rows), 1)
+    sub_rows = lax.broadcasted_iota(jnp.int32, (128, node_rows), 0)
+    loads[0].wait()
+
+    for k in range(peers):
+        live = (lane_rows == turned[:, 8 + k : 9 + k]) & (sub_rows < kept_ref[0, k])
+        picker = jnp.where(live, 1.0, 0.0).astype(BF16)
+        hout[k] = dot(picker, nf_ref[...]).astype(BF16)
+
+    pl.semaphore_wait(pltpu.get_barrier_semaphore(), team - 1 + 2 + len(near_steps))
+    send(hout.at[0], hin.at[0], 8, loop_up)
+    send(hout.at[1], hin.at[1], 8, loop_down)
+    for step in range(1, reps):
+        r_to = lax.rem(rep_at + step, reps)
+        send(hout.at[2 + r_to], hin.at[2 + rep_at], 8, {"loop": loop_at, "rep": r_to})
+    hin[2 + rep_at] = hout[2 + rep_at]
+
+    for step in relay_steps:
+        pl.semaphore_signal(relay_sem, inc=1, device_id=above(step)[1], device_id_type=MESH)
 
     loads[1].wait()
-    loads[2].wait()
+    message, _ = silu_and_slope(dot(nf_ref[...], wm_ref[...]))
+    table[0:blocks] = message.reshape(blocks, 128, 256)
+
+    live_total = count_ref[0, 0]
+    slot_col = lax.broadcasted_iota(jnp.int32, (32, 1), 0)
+    slot_row = lax.broadcasted_iota(jnp.int32, (1, 128), 1)
+    dest_col, source_col = turned[0:32, 0:1], turned[0:32, 1:2]
+    dest_row, source_row = flat[0:1, :], flat[1:2, :]
+
+    def keyed(value, iota):
+        return jnp.where(iota < live_total, value, 64)
+
+    def halo_first(value):
+        return jnp.where(value >= blocks, value - blocks, value + peers)
+
+    forward = slot_order(keyed(dest_col, slot_col), keyed(dest_row, slot_row), (source_col,))
+    backward = slot_order(
+        keyed(halo_first(source_col), slot_col), keyed(halo_first(source_row), slot_row), (dest_col,)
+    )
+    meta_v[...] = jnp.concatenate(forward + backward, axis=0)
+    meta_copy = pltpu.make_async_copy(meta_v, meta_s, meta_sem)
+    meta_copy.start()
+
+    row_at = lax.broadcasted_iota(jnp.int32, (node_rows, 128), 0)
+    lane_at = lax.broadcasted_iota(jnp.int32, (node_rows, 128), 1)
+    for k in range(peers):
+        live = (row_at == rows_ref[k]) & (lane_at < kept_ref[0, k])
+        spread[:, 128 * k : 128 * k + 128] = jnp.where(live, 1.0, 0.0).astype(BF16)
+
+    meta_copy.wait()
+    for load in loads[2:]:
+        load.wait()
+    arrived(hin, 8)
     half_peers = peers // 2
     for first in range(0, peers, half_peers):
         some = slice(first, first + half_peers)
@@ -270,8 +244,6 @@
         table[blocks + first : blocks + first + half_peers] = message.reshape(half_peers, 128, 256)
         halo_slope[some] = gate.reshape(half_peers, 128, 256)
 
-    for load in (loads[0], loads[3], loads[4]):
-        load.wait()
 
     def forward_slots(c, total):
         for lap in range(4):
@@ -283,8 +255,6 @@
 
     lax.fori_loop(0, 6, forward_slots, jnp.zeros((128, 256), F32), unroll=6)
 
-    for load in loads[5:]:
-        load.wait()
 
     def node_update(c, gain_sum):
         at = pl.ds(pl.multiple_of(c * 256, 256), 256)
@@ -339,7 +309,6 @@
         for g in range(plane):
             stage_e[rep * plane + g, 48:64, :] = both
 
-    pl.semaphore_wait(pltpu.get_barrier_semaphore(), team + depth + plane - 1)
     to_team(stage_e, land_e, 0)
 
     @pl.loop(0, node_rows // 256, unroll=2)
@@ -370,12 +339,6 @@
     message_grad += inner_rows(hin[...].reshape(peers * 128, 256), halo_grad[...].reshape(peers * 128, 256))
     deal(stage_l, 0, 1, message_grad)
     to_team(stage_l, land_l, 2)
-
-    row_at = lax.broadcasted_iota(jnp.int32, (node_rows, 128), 0)
-    lane_at = lax.broadcasted_iota(jnp.int32, (node_rows, 128), 1)
-    for k in range(peers):
-        live = (row_at == rows_ref[k]) & (lane_at < kept_ref[0, k])
-        spread[:, 128 * k : 128 * k + 128] = jnp.where(live, 1.0, 0.0).astype(BF16)
 
     arrived(land_e, 0)
     total = added(land_e, team)
@@ -390,6 +353,8 @@
     arrived(land_l, 2)
     lpiece[...] = added(land_l, team).astype(BF16)
     lland[z_at] = lpiece[...]
+
+    pl.semaphore_wait(relay_sem, len(relay_steps))
 
     @pl.loop(1, depth)
     def _(step):
@@ -468,7 +433,7 @@
     collect(out_iw, owned, 16, 2)
     stores[3].start()
 
-    for sem, land in ((0, land_e), (1, rin), (2, land_l), (4, eland), (5, lland), (6, gather_l), (7, gather_e)):
+    for sem, land in ((0, land_e), (1, rin), (2, land_l), (4, eland), (5, lland), (6, gather_l), (7, gather_e), (8, hin)):
         if land.shape[0] > 1:
             copy_all(land.at[1:], send_sem.at[sem]).wait()
     copy_all(pland, send_sem.at[3]).wait()
@@ -528,30 +493,6 @@
     wide = (node_rows, width)
     mega = 1024 * 1024
     rows_in = send_rows.reshape(peers, 1, 128)
-    hin, messages, meta = pl.pallas_call(
-        functools.partial(halo_kernel, reps, loop_size),
-        out_shape=(
-            shape((peers, 128, width), BF16),
-            shape((blocks, 128, width), BF16),
-            shape((8, 128), jnp.int32),
-        ),
-        in_specs=[hbm, hbm, vmem, smem, vmem, smem],
-        out_specs=[hbm, hbm, vmem],
-        scratch_shapes=[
-            pltpu.VMEM(wide, BF16),
-            pltpu.VMEM((width, width), BF16),
-            pltpu.VMEM((128, 128), jnp.int32),
-            pltpu.VMEM((peers, 128, width), BF16),
-            pltpu.VMEM((blocks, 128, width), BF16),
-            pltpu.SemaphoreType.DMA((4,)),
-            pltpu.SemaphoreType.DMA,
-            pltpu.SemaphoreType.DMA,
-        ],
-        compiler_params=pltpu.CompilerParams(
-            collective_id=0, has_side_effects=True, vmem_limit_bytes=56 * mega
-        ),
-        name="halo_rows",
-    )(node_features, message_weight, block_index[0, 0], block_count, rows_in, row_counts[0])
     small = pltpu.VMEM(wide, BF16)
     half = width // reps
     results = (
@@ -566,18 +507,21 @@
     outs = pl.pallas_call(
         functools.partial(layer_kernel, plane, depth, reps, scale),
         out_shape=results,
-        in_specs=[hbm] * 9 + [vmem, smem, vmem, vmem],
+        in_specs=[hbm] * 6 + [vmem, smem, vmem, smem, vmem, vmem],
         out_specs=[hbm] * 7,
         scratch_shapes=[
-            pltpu.VMEM((blocks + peers, 128, width), BF16),
-            pltpu.VMEM((peers, 128, width), BF16),
+            small,
             pltpu.VMEM((width, width), BF16),
-            pltpu.SMEM((8, 128), jnp.int32),
             pltpu.VMEM((slots, 128, 128), BF16),
-            small,
             pltpu.VMEM((2 * width, width), BF16),
             pltpu.VMEM((width, width), BF16),
             small,
+            pltpu.VMEM((128, 128), jnp.int32),
+            pltpu.VMEM((8, 128), jnp.int32),
+            pltpu.SMEM((8, 128), jnp.int32),
+            pltpu.VMEM((peers, 128, width), BF16),
+            pltpu.VMEM((peers, 128, width), BF16),
+            pltpu.VMEM((blocks + peers, 128, width), BF16),
             *(pltpu.VMEM(result.shape, result.dtype) for result in results),
             pltpu.VMEM((peers, 128, width), BF16),
             pltpu.VMEM((peers, 128, width), BF16),
@@ -603,26 +547,27 @@
             pltpu.VMEM((depth, 16 * sub, 128), BF16),
             pltpu.VMEM((16 * sub, 128), BF16),
             pltpu.VMEM((plane, 16 * sub, 128), BF16),
+            pltpu.SemaphoreType.DMA((6,)),
+            pltpu.SemaphoreType.DMA((7,)),
+            pltpu.SemaphoreType.DMA,
+            pltpu.SemaphoreType.REGULAR,
             pltpu.SemaphoreType.DMA((9,)),
-            pltpu.SemaphoreType.DMA((7,)),
-            pltpu.SemaphoreType.DMA((8,)),
-            pltpu.SemaphoreType.DMA((8,)),
+            pltpu.SemaphoreType.DMA((9,)),
         ],
         compiler_params=pltpu.CompilerParams(
-            collective_id=1, has_side_effects=True, vmem_limit_bytes=56 * mega
+            collective_id=0, has_side_effects=True, vmem_limit_bytes=56 * mega
         ),
         name="message_layer",
     )(
-        messages,
-        hin,
+        node_features,
         message_weight,
-        meta,
         adjacency[0, 0],
-        node_features,
         input_weight,
         output_weight,
         cotangent,
-        rows_in,
+        block_index[0, 0],
+        block_count,
+        send_rows.reshape(peers, 1, 128),
         row_counts[0],
         input_bias[None, :],
         norm_gain[None, :],

time: 61.2 us -> 58.1 us (0.949); the launches traced: 60.2 us -> 57.8 us
  Pallas kernels: 58.9 us -> 56.5 us
    pallas_call x1 -> x0, Pallas kernels: 21.8 us -> none  [shards(): pl.pallas_call(functools.partial(halo_kernel, reps, loop_size), out_shape...]
    pallas_call x1, Pallas kernels: 34.8 us -> 54.2 us  [shards(): pl.pallas_call(functools.partial(layer_kernel, plane, depth, reps, scale)...]
where the time goes in v7:
time: 58.1 us; the launch traced here: 57.8 us
  Pallas kernels  56.5 us (97%)
  between operations  1.29 us (2%)
    pallas_call x1, Pallas kernels, shards(): pl.pallas_call(functools.partial(layer_kernel, plane, depth, reps, scale)...  54.2 us
    pallas_call x1, Pallas kernels, shards(): pl.pallas_call(finish_kernel, out_shape=results, in_specs=[hbm] * 7, out_...  2.32 us

profile of v7, /device:TPU:1, one launch (start us, length us, event | category | flops | bytes accessed | tf_op | source)
XLA Modules:
  0.0 57.8 jit_solution(11841923998396345275)
XLA Ops:
  1.3 54.2 %message_layer.1 = (bf16[1024,256]{1,0:T(8,128)(2,1)}, bf16[1024,256]{1,0:T(8,128)(2,1)}, f32[64,256]{1,0:T(8,128)}, f32[128,256]{1,0:T(8,128)}, f32[1,64]{1,0:T...) custom-call(bf16[1024,256]{1,0:T(8,128)(2,1)} %nf_hbm.1, bf16[256,256]{1,0:T(8,128)(2,1)} %wm_hbm.1, ...), custom_call_target="tpu_custom_call" | custom-call | tf_op jit(solution)/shard_map/message_layer/pallas_call | solution.py:507
  55.5 2.3 %write_results.1 = (bf16[1024,256]{1,0:T(8,128)(2,1)}, bf16[1024,256]{1,0:T(8,128)(2,1)}, f32[64,256]{1,0:T(8,128)}, f32[128,256]{1,0:T(8,128)}, f32[1,64]{1,0:T...) custom-call(bf16[1024,256]{1,0:T(8,128)(2,1)} %get-tuple-element.21.refs_0_, bf16[1024,256]{1,0:T(8,128)(2,1)} %get-tuple-element.22.refs_1_, ...), custom_call_target="tpu_custom_call" | custom-call | tf_op jit(solution)/shard_map/write_results/pallas_call | solution.py:575

commit v8 on v7

--- a/solution.py
+++ b/solution.py
@@ -85,9 +85,9 @@
     out_new, out_grad, out_mw, out_iw, out_bias, out_ow, out_gain,
     rout, rin, halo_slope, spread, run,
     agg, hidden, outer_grad, pre_grad, agg_grad, norm_rows, own_grad, halo_grad,
-    stage_e, land_e, psend, pland, epiece, eland, gpiece_e, gather_e,
+    stage_e, core_land, stage_p, land_e, epiece, eland, gpiece_e, gather_e,
     stage_l, land_l, lpiece, lland, gpiece_l, gather_l,
-    load_sem, store_sem, meta_sem, relay_sem, send_sem, recv_sem,
+    load_sem, store_sem, meta_sem, relay_sem, pair_sem, send_sem, recv_sem,
 ):
     sub = 8 // plane
     node_rows = nf_ref.shape[0]
@@ -116,6 +116,16 @@
     parity = lax.rem(z_at, 2)
     z_pair = z_at + 1 - 2 * parity
 
+    core = lax.rem(rep_at, 2)
+    squad = reps * plane
+    squad_at = ((rep_at // 2) * plane + g_at) * 2 + parity
+
+    def comrade(step):
+        other = lax.rem(squad_at + step, squad)
+        z_to = z_at - parity + lax.rem(other, 2)
+        g_to = lax.rem(other // 2, plane)
+        return other, {"loop": z_to * plane + g_to, "rep": other // (2 * plane) * 2 + core}
+
     def twin(step):
         other = lax.rem(parity * plane + g_at + step, 2 * plane)
         z_to, g_to = z_at - parity + other // plane, lax.rem(other, plane)
@@ -146,7 +156,9 @@
 
     def added(land, count):
         total = land[0].astype(F32)
-        return lax.fori_loop(1, count, lambda slot, total: total + land[slot].astype(F32), total)
+        for slot in range(1, count):
+            total = total + land[slot].astype(F32)
+        return total
 
     loads = [
         pltpu.make_async_copy(source, target, load_sem.at[i])
@@ -202,6 +214,9 @@
 
     for step in relay_steps:
         pl.semaphore_signal(relay_sem, inc=1, device_id=above(step)[1], device_id_type=MESH)
+    pl.semaphore_signal(
+        pair_sem, inc=1, device_id={"loop": z_pair * plane + g_at, "rep": rep_at}, device_id_type=MESH
+    )
 
     loads[1].wait()
     message, _ = silu_and_slope(dot(nf_ref[...], wm_ref[...]))
@@ -290,14 +305,14 @@
                     start : start + 16 * tall, half : half + 128
                 ].astype(BF16)
 
-    deal(stage_e, 0, 1, inner_rows(hidden[...], outer_grad[...]))
+    outer_weight = inner_rows(hidden[...], outer_grad[...])
     back_all = pre_grad[...]
     bias_sum = dot(jnp.ones((16, node_rows), BF16), back_all)[0:1]
-    deal(
-        stage_e, 16, 2,
-        jnp.concatenate([inner_rows(nf_ref[...], back_all), inner_rows(agg[...], back_all)], axis=0),
+    inner_weight = jnp.concatenate(
+        [inner_rows(nf_ref[...], back_all), inner_rows(agg[...], back_all)], axis=0
     )
     low_lane = lax.broadcasted_iota(jnp.int32, (1, 128), 1) < 64
+    rows = 24 * sub
     for rep in range(reps):
         at = slice(128 * (rep // 2), 128 * (rep // 2) + 128)
         left, right = bias_sum[:, at], gain_sum[:, at]
@@ -305,11 +320,19 @@
             left = pltpu.roll(left, 64, 1)
         else:
             right = pltpu.roll(right, 64, 1)
-        both = jnp.broadcast_to(jnp.where(low_lane, left, right), (16, 128)).astype(BF16)
+        both = jnp.broadcast_to(jnp.where(low_lane, left, right), (stage_e.shape[2] - rows, 128))
         for g in range(plane):
-            stage_e[rep * plane + g, 48:64, :] = both
-
-    to_team(stage_e, land_e, 0)
+            tiles = []
+            for tile in range(g * sub, (g + 1) * sub):
+                row, half = 16 * (tile // 2), slice(128 * (tile % 2), 128 * (tile % 2) + 128)
+                tiles.append(outer_weight[64 * rep + row : 64 * rep + row + 16, half])
+                tiles.append(inner_weight[128 * rep + 2 * row : 128 * rep + 2 * row + 32, half])
+            block = jnp.concatenate(tiles, axis=0)
+            for part in range(2):
+                slot = ((rep // 2) * plane + g) * 2 + part
+                piece = jnp.concatenate([block[part * rows : (part + 1) * rows], both], axis=0)
+                stage_e[rep % 2, slot] = piece.astype(BF16)
+    send(stage_e.at[1 - core], core_land, 0, {"loop": loop_at, "rep": rep_at + 1 - 2 * core})
 
     @pl.loop(0, node_rows // 256, unroll=2)
     def _(c):
@@ -327,6 +350,17 @@
 
     lax.fori_loop(0, 6, backward_slots, jnp.zeros((128, 256), F32), unroll=6)
 
+    copy_all(core_land, recv_sem.at[0]).wait()
+    stage_p[...] = (stage_e[core].astype(F32) + core_land[...].astype(F32)).astype(BF16)
+    land_e[squad_at] = stage_p[squad_at]
+    pl.semaphore_wait(pair_sem, 1)
+
+    @pl.loop(1, squad)
+    def _(step):
+        other, device = comrade(step)
+        send(stage_p.at[other], land_e.at[squad_at], 3, device)
+
+
     for k in range(peers):
         halo_grad[k] = (run[meta_s[7, k]] * halo_slope[k]).astype(BF16)
     @pl.loop(0, blocks, unroll=4)
@@ -340,21 +374,18 @@
     deal(stage_l, 0, 1, message_grad)
     to_team(stage_l, land_l, 2)
 
-    arrived(land_e, 0)
-    total = added(land_e, team)
-    vec_rows = jnp.broadcast_to(total[48:49], (8, 128))
-    total = jnp.concatenate([total[64 * tile : 64 * tile + 48] for tile in range(sub)], axis=0)
-    rows = 24 * sub
-    for part in range(2):
-        psend[part, 0:rows, :] = total[part * rows : (part + 1) * rows]
-        psend[part, rows:, :] = vec_rows
-    send(psend.at[1 - parity], pland, 3, {"loop": z_pair * plane + g_at, "rep": rep_at})
+    arrived(land_e, 3)
+    pl.semaphore_wait(relay_sem, len(relay_steps))
+    epiece[...] = added(land_e, squad).astype(BF16)
+    eland[z_at // 2] = epiece[...]
+
+    @pl.loop(1, depth // 2)
+    def _(step):
+        send(epiece, eland.at[z_at // 2], 4, above(2 * step)[1])
 
     arrived(land_l, 2)
     lpiece[...] = added(land_l, team).astype(BF16)
     lland[z_at] = lpiece[...]
-
-    pl.semaphore_wait(relay_sem, len(relay_steps))
 
     @pl.loop(1, depth)
     def _(step):
@@ -369,16 +400,6 @@
     for step in range(1, reps):
         r_to = lax.rem(rep_at + step, reps)
         send(rout.at[2 + r_to], rin.at[2 + rep_at], 1, {"loop": loop_at, "rep": r_to})
-
-    copy_all(pland, recv_sem.at[3]).wait()
-    total = psend[parity] + pland[...]
-    filler = jnp.zeros((epiece.shape[0] - total.shape[0], 128), F32)
-    epiece[...] = (jnp.concatenate([total, filler], axis=0) if filler.shape[0] else total).astype(BF16)
-    eland[z_at // 2] = epiece[...]
-
-    @pl.loop(1, depth // 2)
-    def _(step):
-        send(epiece, eland.at[z_at // 2], 4, above(2 * step)[1])
 
     arrived(rin, 1)
     returned = rin[...].reshape(peers * 128, 256)
@@ -433,10 +454,10 @@
     collect(out_iw, owned, 16, 2)
     stores[3].start()
 
-    for sem, land in ((0, land_e), (1, rin), (2, land_l), (4, eland), (5, lland), (6, gather_l), (7, gather_e), (8, hin)):
+    for sem, land in ((1, rin), (2, land_l), (3, land_e), (4, eland), (5, lland), (6, gather_l), (7, gather_e), (8, hin)):
         if land.shape[0] > 1:
             copy_all(land.at[1:], send_sem.at[sem]).wait()
-    copy_all(pland, send_sem.at[3]).wait()
+    copy_all(core_land, send_sem.at[0]).wait()
     for store in stores:
         store.wait()
 
@@ -533,10 +554,10 @@
             pltpu.VMEM(wide, F32),
             small,
             pltpu.VMEM((peers, 128, width), BF16),
-            pltpu.VMEM((reps * plane, 64 * sub, 128), BF16),
-            pltpu.VMEM((reps * plane, 64 * sub, 128), BF16),
-            pltpu.VMEM((2, 24 * sub + 8, 128), F32),
-            pltpu.VMEM((24 * sub + 8, 128), F32),
+            pltpu.VMEM((2, reps * plane, half_rows, 128), BF16),
+            pltpu.VMEM((reps * plane, half_rows, 128), BF16),
+            pltpu.VMEM((reps * plane, half_rows, 128), BF16),
+            pltpu.VMEM((reps * plane, half_rows, 128), BF16),
             pltpu.VMEM((half_rows, 128), BF16),
             pltpu.VMEM((depth // 2, half_rows, 128), BF16),
             pltpu.VMEM((half_rows, 128), BF16),
@@ -550,6 +571,7 @@
             pltpu.SemaphoreType.DMA((6,)),
             pltpu.SemaphoreType.DMA((7,)),
             pltpu.SemaphoreType.DMA,
+            pltpu.SemaphoreType.REGULAR,
             pltpu.SemaphoreType.REGULAR,
             pltpu.SemaphoreType.DMA((9,)),
             pltpu.SemaphoreType.DMA((9,)),

time: 58.1 us -> 55.2 us (0.950)
  Pallas kernels: 56.5 us -> 53.2 us
    pallas_call x1, Pallas kernels: 54.2 us -> 50.9 us  [shards(): pl.pallas_call(functools.partial(layer_kernel, plane, depth, reps, scale)...]
where the time goes in v8:
time: 55.2 us; the launch traced here: 54.5 us
  Pallas kernels  53.2 us (96%)
  between operations  1.29 us (2%)
    pallas_call x1, Pallas kernels, shards(): pl.pallas_call(functools.partial(layer_kernel, plane, depth, reps, scale)...  50.9 us
    pallas_call x1, Pallas kernels, shards(): pl.pallas_call(finish_kernel, out_shape=results, in_specs=[hbm] * 7, out_...  2.32 us

profile of v8, /device:TPU:1, one launch (start us, length us, event | category | flops | bytes accessed | tf_op | source)
XLA Modules:
  0.0 54.5 jit_solution(6222855330238599520)
XLA Ops:
  1.3 50.9 %message_layer.1 = (bf16[1024,256]{1,0:T(8,128)(2,1)}, bf16[1024,256]{1,0:T(8,128)(2,1)}, f32[64,256]{1,0:T(8,128)}, f32[128,256]{1,0:T(8,128)}, f32[1,64]{1,0:T...) custom-call(bf16[1024,256]{1,0:T(8,128)(2,1)} %nf_hbm.1, bf16[256,256]{1,0:T(8,128)(2,1)} %wm_hbm.1, ...), custom_call_target="tpu_custom_call" | custom-call | tf_op jit(solution)/shard_map/message_layer/pallas_call | solution.py:528
  52.2 2.3 %write_results.1 = (bf16[1024,256]{1,0:T(8,128)(2,1)}, bf16[1024,256]{1,0:T(8,128)(2,1)}, f32[64,256]{1,0:T(8,128)}, f32[128,256]{1,0:T(8,128)}, f32[1,64]{1,0:T...) custom-call(bf16[1024,256]{1,0:T(8,128)(2,1)} %get-tuple-element.21.refs_0_, bf16[1024,256]{1,0:T(8,128)(2,1)} %get-tuple-element.22.refs_1_, ...), custom_call_target="tpu_custom_call" | custom-call | tf_op jit(solution)/shard_map/write_results/pallas_call | solution.py:597

commit v9 on v8

--- a/solution.py
+++ b/solution.py
@@ -401,23 +401,14 @@
         r_to = lax.rem(rep_at + step, reps)
         send(rout.at[2 + r_to], rin.at[2 + rep_at], 1, {"loop": loop_at, "rep": r_to})
 
-    arrived(rin, 1)
-    returned = rin[...].reshape(peers * 128, 256)
-
     @pl.loop(0, node_rows // 256, unroll=2)
     def _(c):
         at = pl.ds(pl.multiple_of(c * 256, 256), 256)
         out_new[at, :] = (nf_ref[at, :].astype(F32) + norm_rows[at, :] * gain_ref[...]).astype(BF16)
         total = cot_ref[at, :].astype(F32) + dot_right_t(pre_grad[at, :], wi_ref[0:256, :])
-        total += dot_right_t(own_grad[at, :], wm_ref[...])
-        out_grad[at, :] = (total + dot(spread[at, :], returned)).astype(BF16)
+        norm_rows[at, :] = total + dot_right_t(own_grad[at, :], wm_ref[...])
 
     stores[0].start()
-    stores[1].start()
-
-    arrived(lland, 5)
-    gpiece_l[...] = (added(lland, depth) * scale).astype(BF16)
-    to_plane(gpiece_l, gather_l, 6)
 
     arrived(eland, 4)
     total = added(eland, depth // 2) * scale
@@ -433,6 +424,20 @@
     @pl.loop(1, 2 * plane)
     def _(step):
         send(gpiece_e, gather_e.at[parity * plane + g_at], 7, twin(step))
+
+    arrived(lland, 5)
+    gpiece_l[...] = (added(lland, depth) * scale).astype(BF16)
+    to_plane(gpiece_l, gather_l, 6)
+
+    arrived(rin, 1)
+    returned = rin[...].reshape(peers * 128, 256)
+
+    @pl.loop(0, node_rows // 256, unroll=2)
+    def _(c):
+        at = pl.ds(pl.multiple_of(c * 256, 256), 256)
+        out_grad[at, :] = (norm_rows[at, :] + dot(spread[at, :], returned)).astype(BF16)
+
+    stores[1].start()
 
     def collect(out, owned, first, tall):
         for tile in range(8):

time: 55.2 us -> 54.8 us (level)
  no operation moved by 1% of the time
where the time goes in v9:
time: 54.8 us; the launch traced here: 54 us
  Pallas kernels  52.7 us (96%)
  between operations  1.29 us (2%)
    pallas_call x1, Pallas kernels, shards(): pl.pallas_call(functools.partial(layer_kernel, plane, depth, reps, scale)...  50.4 us
    pallas_call x1, Pallas kernels, shards(): pl.pallas_call(finish_kernel, out_shape=results, in_specs=[hbm] * 7, out_...  2.32 us

profile of v9, /device:TPU:1, one launch (start us, length us, event | category | flops | bytes accessed | tf_op | source)
XLA Modules:
  0.0 54.0 jit_solution(6439832352313122845)
XLA Ops:
  1.3 50.4 %message_layer.1 = (bf16[1024,256]{1,0:T(8,128)(2,1)}, bf16[1024,256]{1,0:T(8,128)(2,1)}, f32[64,256]{1,0:T(8,128)}, f32[128,256]{1,0:T(8,128)}, f32[1,64]{1,0:T...) custom-call(bf16[1024,256]{1,0:T(8,128)(2,1)} %nf_hbm.1, bf16[256,256]{1,0:T(8,128)(2,1)} %wm_hbm.1, ...), custom_call_target="tpu_custom_call" | custom-call | tf_op jit(solution)/shard_map/message_layer/pallas_call | solution.py:533
  51.7 2.3 %write_results.1 = (bf16[1024,256]{1,0:T(8,128)(2,1)}, bf16[1024,256]{1,0:T(8,128)(2,1)}, f32[64,256]{1,0:T(8,128)}, f32[128,256]{1,0:T(8,128)}, f32[1,64]{1,0:T...) custom-call(bf16[1024,256]{1,0:T(8,128)(2,1)} %get-tuple-element.21.refs_0_, bf16[1024,256]{1,0:T(8,128)(2,1)} %get-tuple-element.22.refs_1_, ...), custom_call_target="tpu_custom_call" | custom-call | tf_op jit(solution)/shard_map/write_results/pallas_call | solution.py:602
